TPU v7x, 32 devices: a whole 2x2x4 slice. The times are simulated.
32 devices in a mesh: dp: 16 (over z, y, core), blk: 2 (over x).
Axes of the slice: x: 2, y: 2, z: 4, core: 2. Of those that a mesh axis runs over, the one named last changes fastest.
Arguments:
- tokens: bfloat16 [16, 1024, 768], P('dp', 'blk'), may hold values from -6 to 6
- segments: int32 [16, 1024], P('dp'), may hold values from 0 to 15, never falling along the last dimension, each value on 1 to 198 neighbouring positions
- cotangent: bfloat16 [16, 1024, 768], P('dp', 'blk'), may hold values from -6 to 6
- qkv_weight: float32 [768, 2304], P(('dp', 'blk')), may hold values from -0.21875 to 0.21875
- proj_weight: float32 [768, 768], P(('dp', 'blk')), may hold values from -0.875 to 0.875
- up_weight: float32 [768, 3072], P(('dp', 'blk')), may hold values from -0.21875 to 0.21875
- down_weight: float32 [3072, 768], P(('dp', 'blk')), may hold values from -0.109375 to 0.109375
- vec_params: float32 [12, 768], P(None, ('dp', 'blk')), may hold values from -1.25 to 1.25
- qkv_velocity: float32 [768, 2304], P(('dp', 'blk')), may hold values from -80 to 80
- proj_velocity: float32 [768, 768], P(('dp', 'blk')), may hold values from -40 to 40
- up_velocity: float32 [768, 3072], P(('dp', 'blk')), may hold values from -40 to 40
- down_velocity: float32 [3072, 768], P(('dp', 'blk')), may hold values from -40 to 40
- vec_velocity: float32 [12, 768], P(None, ('dp', 'blk')), may hold values from -80 to 80
- qkv_average: float32 [768, 2304], P(('dp', 'blk')), may hold values from -0.109375 to 0.109375
- proj_average: float32 [768, 768], P(('dp', 'blk')), may hold values from -0.4375 to 0.4375
- up_average: float32 [768, 3072], P(('dp', 'blk')), may hold values from -0.109375 to 0.109375
- down_average: float32 [3072, 768], P(('dp', 'blk')), may hold values from -0.0546875 to 0.0546875
- vec_average: float32 [12, 768], P(None, ('dp', 'blk')), may hold values from -0.625 to 0.625
Outputs:
- output: bfloat16 [16, 1024, 768], P('dp', 'blk')
- tokens_grad: bfloat16 [16, 1024, 768], P('dp', 'blk')
- qkv_grad: float32 [768, 2304], P(('dp', 'blk'))
- proj_grad: float32 [768, 768], P(('dp', 'blk'))
- up_grad: float32 [768, 3072], P(('dp', 'blk'))
- down_grad: float32 [3072, 768], P(('dp', 'blk'))
- vec_grad: float32 [12, 768], P(None, ('dp', 'blk'))
- qkv_master: float32 [768, 2304], P(('dp', 'blk'))
- proj_master: float32 [768, 768], P(('dp', 'blk'))
- up_master: float32 [768, 3072], P(('dp', 'blk'))
- down_master: float32 [3072, 768], P(('dp', 'blk'))
- vec_master: float32 [12, 768], P(None, ('dp', 'blk'))
- qkv_velocity_out: float32 [768, 2304], P(('dp', 'blk'))
- proj_velocity_out: float32 [768, 768], P(('dp', 'blk'))
- up_velocity_out: float32 [768, 3072], P(('dp', 'blk'))
- down_velocity_out: float32 [3072, 768], P(('dp', 'blk'))
- vec_velocity_out: float32 [12, 768], P(None, ('dp', 'blk'))
- qkv_average_out: float32 [768, 2304], P(('dp', 'blk'))
- proj_average_out: float32 [768, 768], P(('dp', 'blk'))
- up_average_out: float32 [768, 3072], P(('dp', 'blk'))
- down_average_out: float32 [3072, 768], P(('dp', 'blk'))
- vec_average_out: float32 [12, 768], P(None, ('dp', 'blk'))
- qkv_copy: bfloat16 [768, 2304], P(('dp', 'blk'))
- proj_copy: bfloat16 [768, 768], P(('dp', 'blk'))
- up_copy: bfloat16 [768, 3072], P(('dp', 'blk'))
- down_copy: bfloat16 [3072, 768], P(('dp', 'blk'))
- vec_copy: bfloat16 [12, 768], P(None, ('dp', 'blk'))
Inputs may be any that keep to these rules, and one draw needn't show every extreme that they name: `segments`: in each row the ids never fall; each image holds 1 to 198 consecutive positions, and some image holds exactly 198; every id from 0 to the largest occurs.
All inputs are finite; a program needn't handle non-finite values.
Results may differ from a plain program's by a relative error of at most 0.014.
Values may be sent and summed in bfloat16 or wider, within the bound.
A program may use at most 256 MiB of HBM per device.

v0:
```python
import math

import jax
import jax.numpy as jnp
from jax import lax
from jax.experimental import pallas as pl
from jax.experimental.pallas import tpu as pltpu
from jax.sharding import PartitionSpec as P

D = 768
HEADS = 12
HEAD_DIM = 64


def layer_norm(value, gain, shift):
    mean = jnp.mean(value, axis=-1, keepdims=True)
    cent = value - mean
    var = jnp.mean(cent * cent, axis=-1, keepdims=True)
    return cent * lax.rsqrt(var + 1e-06) * (1.0 + gain) + shift


def gelu_exact(value):
    return jax.nn.gelu(value, approximate=False)


def contract_tokens(left, right):
    return lax.dot_general(
        left.reshape(-1, left.shape[-1]),
        right.reshape(-1, right.shape[-1]),
        (((0,), (0,)), ((), ())),
        preferred_element_type=jnp.float32,
    )


def times_transpose(left, weight):
    return lax.dot_general(
        left, weight, (((left.ndim - 1,), (1,)), ((), ())), preferred_element_type=jnp.float32
    )


def group_size(rows, block):
    limit = max(1, 512 // block)
    best = 1
    for cand in range(1, rows + 1):
        if rows % cand == 0 and cand <= limit:
            best = cand
    return best


def scores_of(query, keys, seg_query, seg_keys):
    scores = jnp.einsum(
        "gqhd,gkhd->ghqk", query, keys, preferred_element_type=jnp.float32
    ) * HEAD_DIM ** (-0.5)
    allowed = (seg_query[:, :, None] == seg_keys[:, None, :])[:, None]
    return (scores, allowed)


def attend_back(query, kv_all, grad_out, seg_query, segments, group):
    rows, block = (query.shape[0], query.shape[1])
    length = kv_all.shape[1]
    keys = kv_all[0:group, :, :D].reshape(group, length, HEADS, HEAD_DIM)
    values = kv_all[0:group, :, D:].reshape(group, length, HEADS, HEAD_DIM)
    scores, allowed = scores_of(query, keys, seg_query, segments)
    probs = jax.nn.softmax(jnp.where(allowed, scores, -1e30), axis=-1)
    probs_low = probs.astype(jnp.bfloat16)
    prob_grad = jnp.einsum("gqhd,gkhd->ghqk", grad_out, values, preferred_element_type=jnp.float32)
    score_grad = probs * (prob_grad - jnp.sum(probs * prob_grad, axis=-1, keepdims=True))
    score_low = score_grad.astype(jnp.bfloat16)
    dq_part = jnp.einsum(
        "ghqk,gkhd->gqhd", score_low, keys, preferred_element_type=jnp.float32
    ) * HEAD_DIM ** (-0.5)
    dk_part = jnp.einsum(
        "ghqk,gqhd->gkhd", score_low, query, preferred_element_type=jnp.float32
    ) * HEAD_DIM ** (-0.5)
    dv_part = jnp.einsum("ghqk,gqhd->gkhd", probs_low, grad_out, preferred_element_type=jnp.float32)
    dq_parts = dq_part.reshape(group, block, D)
    dkv_parts = jnp.concatenate(
        [dk_part.reshape(group, length, D), dv_part.reshape(group, length, D)], axis=-1
    )
    return (dq_parts, dkv_parts)


def update(weight, grad, velocity, average, rate):
    step_value = grad + 0.0005 * weight
    velocity_new = 0.9 * velocity + step_value
    weight_new = weight - rate * (step_value + 0.9 * velocity_new)
    average_new = 0.9 * average + 0.1 * weight_new
    return (weight_new, velocity_new, average_new)


def on_device(
    tokens,
    segments,
    cotangent,
    qkv_weight,
    proj_weight,
    up_weight,
    down_weight,
    vec_params,
    qkv_velocity,
    proj_velocity,
    up_velocity,
    down_velocity,
    vec_velocity,
    qkv_average,
    proj_average,
    up_average,
    down_average,
    vec_average,
):
    rows, block = (tokens.shape[0], tokens.shape[1])
    length = segments.shape[1]
    total_tokens = rows * lax.axis_size("dp") * length
    rate = 0.05 / math.sqrt(total_tokens)
    group = group_size(rows, block)
    gathered = (
        lax.all_gather(qkv_weight.astype(jnp.bfloat16), ("dp", "blk"), axis=0, tiled=True),
        lax.all_gather(proj_weight.astype(jnp.bfloat16), ("dp", "blk"), axis=0, tiled=True),
        lax.all_gather(up_weight.astype(jnp.bfloat16), ("dp", "blk"), axis=0, tiled=True),
        lax.all_gather(down_weight.astype(jnp.bfloat16), ("dp", "blk"), axis=0, tiled=True),
        lax.all_gather(vec_params.astype(jnp.bfloat16), ("dp", "blk"), axis=1, tiled=True),
    )
    w_query, w_proj, w_up, w_down, vec_low = gathered
    vec = vec_low.astype(jnp.float32)
    bias_up = vec[8:12].reshape(-1)
    position = lax.axis_index("blk")
    seg_query = lax.dynamic_slice_in_dim(segments, position * block, block, 1)
    inputs = tokens.astype(jnp.float32)
    a_one = layer_norm(inputs, vec[0], vec[1]).astype(jnp.bfloat16)
    zero_bias = jnp.zeros_like(vec[2])
    pre = jnp.dot(a_one, w_query, preferred_element_type=jnp.float32) + jnp.concatenate(
        [vec[2], zero_bias, vec[3]]
    )
    qkv = pre.astype(jnp.bfloat16)
    query = qkv[..., :D].reshape(rows, block, HEADS, HEAD_DIM)
    key_value = qkv[..., D:]
    piece = lax.all_gather(key_value, "blk", axis=1, tiled=True)
    top = jnp.full((rows, HEADS, block), -1e30, jnp.float32)
    count = piece.shape[1]
    keys = piece[0:group, :, :D].reshape(group, count, HEADS, HEAD_DIM)
    values = piece[0:group, :, D:].reshape(group, count, HEADS, HEAD_DIM)
    scores, allowed = scores_of(query, keys, seg_query, segments)
    scores = jnp.where(allowed, scores, -1e30)
    new_top = jnp.maximum(top, jnp.max(scores, axis=-1))
    weights = jnp.where(allowed, jnp.exp(scores - new_top[..., None]), 0.0)
    denoms = jnp.sum(weights, axis=-1)
    added = jnp.einsum(
        "ghqk,gkhd->gqhd", weights.astype(jnp.bfloat16), values, preferred_element_type=jnp.float32
    )
    mixed = (added / jnp.transpose(denoms, (0, 2, 1))[..., None]).reshape(rows, block, D)
    mixed_low = mixed.astype(jnp.bfloat16)
    second = inputs + jnp.dot(mixed_low, w_proj, preferred_element_type=jnp.float32) + vec[4]
    second_norm, norm_two_back = jax.vjp(layer_norm, second, vec[5], vec[6])
    a_two = second_norm.astype(jnp.bfloat16)
    hidden = jnp.dot(a_two, w_up, preferred_element_type=jnp.float32) + bias_up
    act_value, gelu_back = jax.vjp(gelu_exact, hidden)
    act = act_value.astype(jnp.bfloat16)
    result = second + jnp.dot(act, w_down, preferred_element_type=jnp.float32) + vec[7]
    output = result.astype(jnp.bfloat16)
    out_grad = cotangent.astype(jnp.float32)
    grad_down = contract_tokens(act, cotangent)
    bias_down_grad = jnp.sum(out_grad, axis=(0, 1))
    act_grad = times_transpose(cotangent, w_down)
    hidden_grad = gelu_back(act_grad)[0].astype(jnp.bfloat16)
    bias_up_grad = jnp.sum(hidden_grad.astype(jnp.float32), axis=(0, 1))
    grad_up = contract_tokens(a_two, hidden_grad)
    a_two_grad = times_transpose(hidden_grad, w_up)
    second_part, gain_two_grad, shift_two_grad = norm_two_back(a_two_grad)
    second_grad = out_grad + second_part
    attn_grad = second_grad.astype(jnp.bfloat16)
    bias_proj_grad = jnp.sum(attn_grad.astype(jnp.float32), axis=(0, 1))
    grad_proj = contract_tokens(mixed_low, attn_grad)
    mixed_grad = (
        times_transpose(attn_grad, w_proj)
        .astype(jnp.bfloat16)
        .reshape(rows, block, HEADS, HEAD_DIM)
    )
    kv_again = lax.all_gather(key_value, "blk", axis=1, tiled=True)
    query_grad, kv_terms = attend_back(query, kv_again, mixed_grad, seg_query, segments, group)
    kv_grad = lax.psum_scatter(
        kv_terms.astype(jnp.bfloat16), "blk", scatter_dimension=1, tiled=True
    ).astype(jnp.float32)
    qkv_grad_low = jnp.concatenate([query_grad, kv_grad], axis=-1).astype(jnp.bfloat16)
    qkv_sums = jnp.sum(qkv_grad_low.astype(jnp.float32), axis=(0, 1))
    grad_query = contract_tokens(a_one, qkv_grad_low)
    a_one_grad = times_transpose(qkv_grad_low, w_query)
    norm_one_back = jax.vjp(layer_norm, inputs, vec[0], vec[1])[1]
    first_part, gain_one_grad, shift_one_grad = norm_one_back(a_one_grad)
    tokens_grad = (second_grad + first_part).astype(jnp.bfloat16)
    vec_local = jnp.concatenate(
        [
            jnp.stack(
                [
                    gain_one_grad,
                    shift_one_grad,
                    qkv_sums[:D],
                    qkv_sums[2 * D :],
                    bias_proj_grad,
                    gain_two_grad,
                    shift_two_grad,
                    bias_down_grad,
                ]
            ),
            bias_up_grad.reshape(4, D),
        ],
        axis=0,
    )
    query_share, proj_share, up_share, down_share, vec_share = (
        lax.psum_scatter(grad_query, ("dp", "blk"), scatter_dimension=0, tiled=True),
        lax.psum_scatter(grad_proj, ("dp", "blk"), scatter_dimension=0, tiled=True),
        lax.psum_scatter(grad_up, ("dp", "blk"), scatter_dimension=0, tiled=True),
        lax.psum_scatter(grad_down, ("dp", "blk"), scatter_dimension=0, tiled=True),
        lax.psum_scatter(vec_local, ("dp", "blk"), scatter_dimension=1, tiled=True),
    )
    qkv_new = update(qkv_weight, query_share, qkv_velocity, qkv_average, rate)
    proj_new = update(proj_weight, proj_share, proj_velocity, proj_average, rate)
    up_new = update(up_weight, up_share, up_velocity, up_average, rate)
    down_new = update(down_weight, down_share, down_velocity, down_average, rate)
    vec_new = update(vec_params, vec_share, vec_velocity, vec_average, rate)
    return (
        output,
        tokens_grad,
        query_share,
        proj_share,
        up_share,
        down_share,
        vec_share,
        qkv_new[0],
        proj_new[0],
        up_new[0],
        down_new[0],
        vec_new[0],
        qkv_new[1],
        proj_new[1],
        up_new[1],
        down_new[1],
        vec_new[1],
        qkv_new[2],
        proj_new[2],
        up_new[2],
        down_new[2],
        vec_new[2],
        qkv_new[0].astype(jnp.bfloat16),
        proj_new[0].astype(jnp.bfloat16),
        up_new[0].astype(jnp.bfloat16),
        down_new[0].astype(jnp.bfloat16),
        vec_new[0].astype(jnp.bfloat16),
    )


PIECE = (48, 384)
NP = 12
Z, Y, X, C = 4, 2, 2, 2
AHEAD = 2
REACH = 256
TILE = 128
SPAN = TILE + 2 * REACH
PAIRS = HEADS // 2
MESH = pl.DeviceIdType.MESH
F32, BF16 = jnp.float32, jnp.bfloat16
NT = (((1,), (1,)), ((), ()))
TN = (((0,), (0,)), ((), ()))


def place():
    d, x = lax.axis_index("dp"), lax.axis_index("blk")
    return d // (2 * Y), (d // 2) % Y, d % 2, x


def ident(z, y, c, x):
    return ((z * Y + y) * 2 + c, x)


def greet(z, y, c, x):
    barrier = pltpu.get_barrier_semaphore()
    peers = [ident((z + k) % Z, y, c, x) for k in range(1, Z)]
    peers += [ident(z, 1 - y, c, x), ident(z, y, c, 1 - x), ident(z, y, 1 - c, x)]
    for peer in peers:
        pl.semaphore_signal(barrier, inc=1, device_id=peer, device_id_type=MESH)
    pl.semaphore_wait(barrier, len(peers))


def remote(src, dst, send, recv, peer):
    return pltpu.make_async_remote_copy(
        src_ref=src, dst_ref=dst, send_sem=send, recv_sem=recv, device_id=peer, device_id_type=MESH
    )


def begin(copies):
    for copy in copies:
        copy.start()


def arrive(copies):
    for copy in copies:
        copy.wait_recv()


def within(index, low, high, run):
    if isinstance(index, int):
        if low <= index < high:
            run()
    else:
        pl.when(jnp.logical_and(index >= low, index < high))(run)


def loop(count, body):
    def step(i, carry):
        body(i)
        return carry

    lax.fori_loop(0, count, step, 0)


def cols(j, width):
    return pl.ds(pl.multiple_of(j * width, width), width)


def dot(a, b, dims=None):
    dims = (((1,), (0,)), ((), ())) if dims is None else dims
    return lax.dot_general(a, b, dims, preferred_element_type=F32)


class Vec:
    def __init__(self, at, now, got, send, recv):
        self.at, self.now, self.got, self.send, self.recv = at, now, got, send, recv

    def copies(self, step):
        z, y, c, x = self.at
        peers = [
            [ident(z, y, 1 - c, x)],
            [ident(z, y, c, 1 - x)],
            [ident(z, 1 - y, c, x)],
            [ident((z + k) % Z, y, c, x) for k in range(1, Z)],
        ][step]
        return [
            remote(self.now.at[step], self.got.at[step + k], self.send.at[step + k], self.recv.at[step + k], peer)
            for k, peer in enumerate(peers)
        ]

    def begin(self, step):
        begin(self.copies(step))

    def total(self, step):
        copies = self.copies(step)
        arrive(copies)
        total = self.now[step]
        for k in range(len(copies)):
            total = total + self.got[step + k]
        return total

    def sent(self):
        for step in range(4):
            for copy in self.copies(step):
                copy.wait_send()


def normal(value):
    mean = jnp.mean(value, axis=-1, keepdims=True)
    cent = value - mean
    var = jnp.mean(cent * cent, axis=-1, keepdims=True)
    scale = lax.rsqrt(var + 1e-06)
    return cent * scale, scale


def window(tile, x):
    first = jnp.where(x == 0, jnp.maximum(tile - 2, 0), jnp.minimum(tile, 1))
    return pl.ds(pl.multiple_of(first * TILE, TILE), SPAN)


def mask_fill(seg_col, seg_row, bias, x, tiles):
    def one(tile):
        column = seg_col[window(tile, x), :]
        row = seg_row[0:1, cols(tile, TILE)]
        bias[tile] = jnp.where(column == row, 0.0, -1e30).astype(F32)

    loop(tiles, one)


def split_heads(pair_block):
    lane = lax.broadcasted_iota(jnp.int32, pair_block.shape, 1)
    zero = jnp.zeros_like(pair_block)
    return jnp.concatenate(
        [jnp.where(lane < HEAD_DIM, pair_block, zero), jnp.where(lane < HEAD_DIM, zero, pair_block)], axis=0
    )


def join_heads(both):
    own = jnp.concatenate([both[:HEAD_DIM, :TILE], both[HEAD_DIM:, TILE:]], axis=0)
    return jnp.transpose(own)


def rows_from_stage(stage, target, col):
    def group(g):
        parts = [stage[c, g % Y, x, g // Y].astype(F32) for c in range(C) for x in range(X)]
        rows = pl.ds(pl.multiple_of(g * 96, 96), 96)
        target[rows, col : col + 384] = jnp.concatenate([p[:24] for p in parts], axis=0).astype(BF16)
        target[rows, col + 384 : col + 768] = jnp.concatenate([p[24:] for p in parts], axis=0).astype(BF16)

    loop(Z * Y, group)


def down_from_stage(stage, target, half, col):
    def group(g):
        for c in range(C):
            for x in range(X):
                start = pl.multiple_of(g * 384 + (c * X + x) * 96 + half * 48, 16)
                target[pl.ds(start, 48), col * 384 : col * 384 + 384] = stage[c, g % Y, x, g // Y]

    loop(Z * Y, group)


class Gather:
    def __init__(self, at, unit, full, own, send, recv):
        self.at, self.unit, self.full, self.own, self.send, self.recv = at, unit, full, own, send, recv

    def mine(self, t):
        z, y, c, x = self.at
        return pltpu.make_async_copy(self.unit.at[t], self.full.at[c, y, x, z, t], self.own.at[t])

    def first(self, t):
        z, y, c, x = self.at
        return [
            remote(
                self.unit.at[t], self.full.at[c, y, x, z, t], self.send.at[t, k - 1], self.recv.at[t, k - 1],
                ident((z + k) % Z, y, c, x),
            )
            for k in range(1, Z)
        ]

    def second(self, t):
        z, y, c, x = self.at
        low, high = self.full.at[c, y, x, 0:2, t], self.full.at[c, y, x, 2:4, t]
        return [
            remote(low, low, self.send.at[t, 3], self.recv.at[t, 3], ident(z, y, c, 1 - x)),
            remote(high, high, self.send.at[t, 4], self.recv.at[t, 4], ident(z, 1 - y, c, x)),
        ]

    def third(self, t):
        z, y, c, x = self.at
        low, high = self.full.at[c, y, :, 0:2, t], self.full.at[c, :, x, 2:4, t]
        return [
            remote(low, low, self.send.at[t, 5], self.recv.at[t, 5], ident(z, 1 - y, c, x)),
            remote(high, high, self.send.at[t, 6], self.recv.at[t, 6], ident(z, y, c, 1 - x)),
        ]

    def last(self, t):
        z, y, c, x = self.at
        block = self.full.at[c, :, :, :, t]
        return [remote(block, block, self.send.at[t, 7], self.recv.at[t, 7], ident(z, y, 1 - c, x))]

    def start(self):
        loop(NP, lambda t: self.mine(t).start())
        loop(AHEAD, lambda t: begin(self.first(t)))

    def progress(self, i):
        def to_second():
            self.mine(i).wait()
            arrive(self.first(i))
            begin(self.second(i))

        def to_third():
            arrive(self.second(i - 1))
            begin(self.third(i - 1))

        def to_last():
            arrive(self.third(i - 2))
            begin(self.last(i - 2))

        within(i, 0, NP, to_second)
        within(i, 1, NP + 1, to_third)
        within(i, 2, NP + 2, to_last)
        within(i, 0, NP - AHEAD, lambda: begin(self.first(i + AHEAD)))

    def sent(self):
        def one(t):
            for copy in self.first(t) + self.second(t) + self.third(t) + self.last(t):
                copy.wait_send()

        loop(NP, one)


def forward_kernel(
    unit, vec_in, tok, seg_col, seg_row,
    full, vec_out, out_o, q_o, k_o, v_o, o_o, stat_o, x2_o, a2_o, z_o, slope_o,
    near, a1, wbig, wdown, stage, vecf, bias, out_s, q_s, k_s, v_s, o_s, stat_s, x2_s, a2_s, z_s, slope_s,
    vec_now, vec_got, own, send, recv, vsend, vrecv, hsem, ssem, osem,
):
    z, y, c, x = at = place()
    block = tok.shape[0]
    tiles = block // TILE
    offset = pl.multiple_of(x * REACH, REACH)
    vec_now[0] = vec_in[...]
    greet(*at)
    gather = Gather(at, unit, full, own, send, recv)
    gather.start()
    vec = Vec(at, vec_now, vec_got, vsend, vrecv)
    vec.begin(0)
    away = pl.multiple_of((1 - x) * REACH, REACH)
    land = pl.multiple_of(x * block, REACH)
    halo = remote(
        tok.at[pl.ds(away, REACH)], near.at[pl.ds(land, REACH)], hsem.at[0], hsem.at[1], ident(z, y, c, 1 - x)
    )
    halo.start()
    near[pl.ds(offset, block), :] = tok[...]

    def put(k, src, dst):
        return pltpu.make_async_copy(src, dst, osem.at[k])

    def vec_step(step):
        total = vec.total(step)
        if step < 3:
            vec_now[step + 1] = total
            vec.begin(step + 1)
        else:
            vec_out[...] = total
            vecf[...] = total.astype(F32)

    def load(t):
        arrive(gather.last(t))
        copy = pltpu.make_async_copy(full.at[:, :, :, :, t], stage, ssem)
        copy.start()
        copy.wait()

    vec_step(0)
    vec_step(1)
    gather.progress(0)
    vec_step(2)
    vec_step(3)
    gather.progress(1)
    halo.wait_recv()

    def norm_one(i):
        rows = pl.ds(pl.multiple_of(i * 256, 256), 256)
        value = normal(near[rows, :].astype(F32))[0]
        a1[rows, :] = (value * (1.0 + vecf[0:1, :]) + vecf[1:2, :]).astype(BF16)

    loop(near.shape[0] // 256, norm_one)
    mask_fill(seg_col, seg_row, bias, x, tiles)
    gather.progress(2)
    gather.progress(3)
    load(0)
    rows_from_stage(stage, wbig, D)

    def keys(j):
        k_s[:, cols(j, 256)] = dot(a1[...], wbig[:, pl.ds(pl.multiple_of(D + j * 256, 256), 256)]).astype(BF16)

    loop(3, keys)
    gather.progress(4)
    load(1)
    rows_from_stage(stage, wbig, 2 * D)

    def values(j):
        value = dot(a1[...], wbig[:, pl.ds(pl.multiple_of(2 * D + j * 256, 256), 256)])
        v_s[:, cols(j, 256)] = (value + vecf[3:4, cols(j, 256)]).astype(BF16)

    loop(3, values)
    load(2)
    rows_from_stage(stage, wbig, 0)

    def queries(j):
        value = dot(a1[pl.ds(offset, block), :], wbig[:, cols(j, 256)]) + vecf[2:3, cols(j, 256)]
        q_s[:, cols(j, 256)] = value.astype(BF16) * HEAD_DIM ** (-0.5)

    loop(3, queries)
    put(0, k_s, k_o).start()
    put(1, v_s, v_o).start()
    put(2, q_s, q_o).start()

    def attend(pair):
        gather.progress(pair + 5)
        lanes = cols(pair, 128)

        def one(tile):
            rows = cols(tile, TILE)
            span = window(tile, x)
            both = split_heads(q_s[rows, lanes])
            fill = bias[tile]
            scores = dot(k_s[span, lanes], both, NT) + jnp.concatenate([fill, fill], axis=1)
            top = jnp.max(scores, axis=0, keepdims=True)
            weights = jnp.exp(scores - top)
            total = jnp.sum(weights, axis=0, keepdims=True)
            mixed = dot(v_s[span, lanes], weights.astype(BF16), TN) / total
            o_s[rows, lanes] = join_heads(mixed).astype(BF16)
            stat_s[pair * tiles + tile] = jnp.broadcast_to(top + jnp.log(total), (8, 2 * TILE))

        loop(tiles, one)

    loop(PAIRS, attend)
    put(3, o_s, o_o).start()
    put(4, stat_s, stat_o).start()
    load(3)
    rows_from_stage(stage, wbig, 3 * D)

    def project(j):
        value = dot(o_s[...], wbig[:, pl.ds(pl.multiple_of(3 * D + j * 256, 256), 256)])
        x2_s[:, cols(j, 256)] = tok[:, cols(j, 256)].astype(F32) + value + vecf[4:5, cols(j, 256)]

    loop(3, project)

    def norm_two(i):
        rows = pl.ds(pl.multiple_of(i * 256, 256), 256)
        value = normal(x2_s[rows, :])[0]
        a2_s[rows, :] = (value * (1.0 + vecf[5:6, :]) + vecf[6:7, :]).astype(BF16)

    loop(block // 256, norm_two)
    put(5, x2_s, x2_o).start()
    put(6, a2_s, a2_o).start()
    gather.progress(11)

    def expand(j):
        col = pl.multiple_of(j * 256, 256)
        u = dot(a2_s[...], wbig[:, pl.ds(pl.multiple_of(4 * D + col, 256), 256)])
        u = u + vecf[pl.ds(8 + j // 3, 1), pl.ds(pl.multiple_of((j % 3) * 256, 256), 256)]
        half = 0.5 + 0.5 * lax.erf(u * math.sqrt(0.5))
        z_s[:, cols(j, 256)] = (u * half).astype(BF16)
        slope = half + u * (jnp.exp(-0.5 * u * u) * (1.0 / math.sqrt(2.0 * math.pi)))
        slope_s[:, cols(j, 256)] = slope.astype(BF16)

    for t in range(4):
        load(4 + t)
        rows_from_stage(stage, wbig, (4 + t) * D)
        loop(3, lambda j: expand(j + 3 * t))
        if t == 1:
            gather.progress(12)
    put(7, z_s, z_o).start()
    put(8, slope_s, slope_o).start()
    gather.progress(13)
    for t in range(4):
        load(8 + t)
        down_from_stage(stage, wdown, t % 2, t // 2)
        if t % 2 == 1:
            col = slice(t // 2 * 384, t // 2 * 384 + 384)
            value = dot(z_s[...], wdown[:, col])
            out_s[:, col] = (x2_s[:, col] + value + vecf[7:8, col]).astype(BF16)
    put(9, out_s, out_o).start()
    pairs = [(k_s, k_o), (v_s, v_o), (q_s, q_o), (o_s, o_o), (stat_s, stat_o), (x2_s, x2_o), (a2_s, a2_o)]
    for k, (src, dst) in enumerate(pairs + [(z_s, z_o), (slope_s, slope_o), (out_s, out_o)]):
        put(k, src, dst).wait()
    gather.sent()
    vec.sent()
    halo.wait_send()


def forward_all(unit, vec_placed, tok, seg_col, seg_row):
    block, near = tok.shape[0], seg_col.shape[0]
    ff = 4 * D
    tiles = block // TILE
    shapes = [
        ((block, D), BF16),
        ((block, D), BF16),
        ((near, D), BF16),
        ((near, D), BF16),
        ((block, D), BF16),
        ((PAIRS * tiles, 8, 2 * TILE), F32),
        ((block, D), F32),
        ((block, D), BF16),
        ((block, ff), BF16),
        ((block, ff), BF16),
    ]
    hbm, vmem = pl.BlockSpec(memory_space=pl.ANY), pl.BlockSpec(memory_space=pltpu.VMEM)
    outs = [((C, Y, X, Z, NP) + PIECE, BF16), (vec_placed.shape, BF16)] + shapes
    return pl.pallas_call(
        forward_kernel,
        out_shape=tuple(jax.ShapeDtypeStruct(*one) for one in outs),
        in_specs=[vmem] * 5,
        out_specs=tuple([hbm, vmem] + [hbm] * len(shapes)),
        scratch_shapes=[
            pltpu.VMEM((near, D), BF16),
            pltpu.VMEM((near, D), BF16),
            pltpu.VMEM((D, 8 * D), BF16),
            pltpu.VMEM((ff, D), BF16),
            pltpu.VMEM((C, Y, X, Z) + PIECE, BF16),
            pltpu.VMEM(vec_placed.shape, F32),
            pltpu.VMEM((tiles, SPAN, TILE), F32),
            *[pltpu.VMEM(*one) for one in shapes],
            pltpu.VMEM((4,) + vec_placed.shape, BF16),
            pltpu.VMEM((6,) + vec_placed.shape, BF16),
            pltpu.SemaphoreType.DMA((NP,)),
            pltpu.SemaphoreType.DMA((NP, 8)),
            pltpu.SemaphoreType.DMA((NP, 8)),
            pltpu.SemaphoreType.DMA((6,)),
            pltpu.SemaphoreType.DMA((6,)),
            pltpu.SemaphoreType.DMA((2,)),
            pltpu.SemaphoreType.DMA,
            pltpu.SemaphoreType.DMA((10,)),
        ],
        compiler_params=pltpu.CompilerParams(
            collective_id=0, has_side_effects=True, vmem_limit_bytes=60 << 20
        ),
        name="forward_all",
    )(unit, vec_placed, tok, seg_col, seg_row)


def to_unit(qkv, proj, up, down):
    def split(weight):
        rows, width = weight.shape
        count = width // 768
        return weight.reshape(rows, count, 2, 384).transpose(1, 2, 0, 3).reshape(count, 48, 384)

    three = split(qkv)
    four = down.reshape(2, 48, 2, 384).transpose(2, 0, 1, 3).reshape(4, 48, 384)
    return jnp.concatenate([three[1:], three[:1], split(proj), split(up), four], axis=0)


class Scatter:
    def __init__(self, at, local, got_core, got_two, got_one, got_z, out, send, recv):
        self.at, self.local, self.out, self.send, self.recv = at, local, out, send, recv
        self.got = got_core, got_two, got_one, got_z

    def core(self, t):
        z, y, c, x = self.at
        peer = ident(z, y, 1 - c, x)
        return [remote(self.local.at[1 - c, :, :, :, t], self.got[0].at[t], self.send.at[t, 0], self.recv.at[t, 0], peer)]

    def two(self, t):
        z, y, c, x = self.at
        low, high = self.local.at[c, 1 - y, :, 0:2, t], self.local.at[c, :, 1 - x, 2:4, t]
        return [
            remote(low, self.got[1].at[t, 0], self.send.at[t, 1], self.recv.at[t, 1], ident(z, 1 - y, c, x)),
            remote(high, self.got[1].at[t, 1], self.send.at[t, 2], self.recv.at[t, 2], ident(z, y, c, 1 - x)),
        ]

    def one(self, t):
        z, y, c, x = self.at
        low, high = self.local.at[c, y, 1 - x, 0:2, t], self.local.at[c, 1 - y, x, 2:4, t]
        return [
            remote(low, self.got[2].at[t, 0], self.send.at[t, 3], self.recv.at[t, 3], ident(z, y, c, 1 - x)),
            remote(high, self.got[2].at[t, 1], self.send.at[t, 4], self.recv.at[t, 4], ident(z, 1 - y, c, x)),
        ]

    def along(self, t):
        z, y, c, x = self.at
        return [
            remote(
                self.local.at[c, y, x, (z + k) % Z, t], self.got[3].at[t, k - 1], self.send.at[t, 4 + k],
                self.recv.at[t, 4 + k], ident((z + k) % Z, y, c, x),
            )
            for k in range(1, Z)
        ]

    def add(self, where, value):
        self.local[where] = (self.local[where].astype(F32) + value.astype(F32)).astype(BF16)

    def after_core(self, t):
        c = self.at[2]
        arrive(self.core(t))
        for a in range(Y):
            for b in range(X):
                self.add((c, a, b, slice(None), t), self.got[0][t, a, b])
        begin(self.two(t))

    def after_two(self, t):
        z, y, c, x = self.at
        arrive(self.two(t))
        for b in range(2):
            self.add((c, y, b, slice(0, 2), t), self.got[1][t, 0, b])
            self.add((c, b, x, slice(2, 4), t), self.got[1][t, 1, b])
        begin(self.one(t))

    def after_one(self, t):
        z, y, c, x = self.at
        arrive(self.one(t))
        for b in range(2):
            self.add((c, y, x, slice(2 * b, 2 * b + 2), t), self.got[2][t, b])
        begin(self.along(t))

    def after_z(self, t):
        z, y, c, x = self.at
        arrive(self.along(t))
        total = self.local[c, y, x, z, t].astype(F32)
        for k in range(Z - 1):
            total = total + self.got[3][t, k].astype(F32)
        self.out[t] = total

    def progress(self, i):
        within(i, 0, NP, lambda: self.after_core(i))
        within(i, 1, NP + 1, lambda: self.after_two(i - 1))
        within(i, 2, NP + 2, lambda: self.after_one(i - 2))
        within(i, 3, NP + 3, lambda: self.after_z(i - 3))

    def sent(self):
        def each(t):
            for copy in self.core(t) + self.two(t) + self.one(t) + self.along(t):
                copy.wait_send()

        loop(NP, each)


def total_rows(value):
    return jnp.sum(value.astype(F32), axis=0, keepdims=True)


def norm_back(value, grad, gain):
    unit_value, scale = normal(value)
    inner = grad * (1.0 + gain)
    mean_one = jnp.mean(inner, axis=-1, keepdims=True)
    mean_two = jnp.mean(inner * unit_value, axis=-1, keepdims=True)
    back = scale * (inner - mean_one - unit_value * mean_two)
    return back, total_rows(grad * unit_value), total_rows(grad)


def backward_kernel(
    full, vec_in, tok_o, dy_o, seg_col, seg_row, q_o, k_o, v_o, o_o, stat_o, x2_o, a2_o, z_o, slope_o,
    out, vec_out, tok_grad,
    local, got_core, got_two, got_one, got_z, wbuf, stage, bias, vecf, tok, dy, q_s, k_s, v_s, o_s, stat_s, x2_s, a2_s, z_s,
    slope_s, dx, da, acc_k, acc_v, halo_s, halo_r, vec_now, vec_got, send, recv, vsend, vrecv, hsend, hrecv, isem, ssem,
):
    z, y, c, x = at = place()
    block = tok.shape[0]
    tiles = block // TILE
    offset = pl.multiple_of(x * REACH, REACH)
    away = pl.multiple_of((1 - x) * REACH, REACH)
    outside = pl.multiple_of((1 - x) * block, REACH)
    order = [8, 9, 10, 11, 4, 5, 6, 7, 3, 2, 0, 1]

    def fetch(n):
        return pltpu.make_async_copy(full.at[:, :, :, :, order[n]], stage.at[n % 2], ssem.at[n % 2])

    def take(n, use):
        fetch(n).wait()
        use(stage.at[n % 2])
        if n + 2 < NP:
            fetch(n + 2).start()

    pairs = [
        (z_o, z_s), (dy_o, dy), (slope_o, slope_s), (a2_o, a2_s), (x2_o, x2_s), (o_o, o_s), (k_o, k_s), (v_o, v_s),
        (q_o, q_s), (stat_o, stat_s), (tok_o, tok),
    ]

    def inward(k):
        return pltpu.make_async_copy(pairs[k][0], pairs[k][1], isem.at[k])

    for k in range(2):
        inward(k).start()
    for n in range(2):
        fetch(n).start()
    for k in range(2, len(pairs)):
        inward(k).start()
    greet(*at)
    scatter = Scatter(at, local, got_core, got_two, got_one, got_z, out, send, recv)
    vec = Vec(at, vec_now, vec_got, vsend, vrecv)
    vec_now[0] = jnp.zeros(vec_now.shape[1:], F32)
    vecf[...] = vec_in[...].astype(F32)

    def gain_row(row, where, value):
        vec_now[0, row : row + 1, where] = vec_now[0, row : row + 1, where] + value

    def weight_grad(left, right, t):
        def half(h):
            value = dot(left[:, cols(h, 384)], right[...], TN)
            for g in range(4):
                for k in range(4):
                    part = value[g * 96 + k * 24 : g * 96 + k * 24 + 24]
                    part = jnp.concatenate([part[:, :384], part[:, 384:]], axis=0).astype(BF16)
                    local[k // 2, g % 2, k % 2, 2 * h + g // 2, t] = part

        loop(2, half)
        begin(scatter.core(t))

    inward(0).wait()
    inward(1).wait()
    for col in range(2):
        def down_grad(g):
            value = dot(z_s[:, cols(g, 384)], dy[:, col * 384 : col * 384 + 384], TN).astype(BF16)
            for k in range(4):
                for half in range(2):
                    part = value[k * 96 + half * 48 : k * 96 + half * 48 + 48]
                    local[k // 2, g % Y, k % 2, g // Y, 2 * col + half] = part

        loop(Z * Y, down_grad)
        begin(scatter.core(2 * col))
        begin(scatter.core(2 * col + 1))
    gain_row(7, slice(None), total_rows(dy[...]))
    mask_fill(seg_col, seg_row, bias, x, tiles)
    for n in range(4):
        take(n, lambda part: down_from_stage(part, wbuf, n % 2, n // 2))
    inward(2).wait()
    scatter.progress(0)

    def hidden(n):
        rows = pl.ds(pl.multiple_of(n * 256, 256), 256)
        grad = dot(dy[...], wbuf[rows, :], NT) * slope_s[:, cols(n, 256)].astype(F32)
        low = grad.astype(BF16)
        slope_s[:, cols(n, 256)] = low
        where = pl.ds(pl.multiple_of((n % 3) * 256, 256), 256)
        vec_now[0, pl.ds(8 + n // 3, 1), where] = total_rows(low)

    loop(12, hidden)
    scatter.progress(1)
    inward(3).wait()
    for t in range(4):
        weight_grad(a2_s, slope_s.at[:, t * D : t * D + D], 4 + t)
    scatter.progress(2)
    for n in range(4, 8):
        take(n, lambda part: rows_from_stage(part, wbuf.at[pl.ds((n - 4) * D, D)], 0))

    def inner_grad(n):
        value = None
        for t in range(4):
            rows = pl.ds(pl.multiple_of(t * D + n * 256, 256), 256)
            part = dot(slope_s[:, t * D : t * D + D], wbuf[rows, :], NT)
            value = part if value is None else value + part
        dx[:, cols(n, 256)] = value

    loop(3, inner_grad)
    inward(4).wait()

    def norm_two(i):
        rows = cols(i, 128)
        grad = dx[rows, :]
        back, gain, shift = norm_back(x2_s[rows, :], grad, vecf[5:6, :])
        total = dy[rows, :].astype(F32) + back
        low = total.astype(BF16)
        dx[rows, :] = total
        da[rows, :] = low
        gain_row(5, slice(None), gain)
        gain_row(6, slice(None), shift)
        gain_row(4, slice(None), total_rows(low))

    loop(block // 128, norm_two)
    inward(5).wait()
    weight_grad(o_s, da, 8)
    take(8, lambda part: rows_from_stage(part, wbuf.at[pl.ds(3 * D, D)], 0))

    def mixed_grad(n):
        rows = pl.ds(pl.multiple_of(3 * D + n * 256, 256), 256)
        o_s[:, cols(n, 256)] = dot(da[...], wbuf[rows, :], NT).astype(BF16)

    loop(3, mixed_grad)
    scatter.progress(3)
    for k in range(6, 11):
        inward(k).wait()

    def halo(pair):
        return remote(halo_s.at[pair], halo_r.at[pair], hsend.at[pair], hrecv.at[pair], ident(z, y, c, 1 - x))

    def attend(pair):
        lanes = cols(pair, 128)
        pl.when(pair % 2 == 1)(lambda: scatter.progress(4 + pair // 2))
        acc_k[...] = jnp.zeros(acc_k.shape, F32)
        acc_v[...] = jnp.zeros(acc_v.shape, F32)

        def each(tile):
            rows = cols(tile, TILE)
            span = window(tile, x)
            both, grads = split_heads(q_s[rows, lanes]), split_heads(o_s[rows, lanes])
            fill = bias[tile]
            scores = dot(k_s[span, lanes], both, NT) + jnp.concatenate([fill, fill], axis=1)
            probs = jnp.exp(scores - stat_s[pair * tiles + tile][0:1])
            low = probs.astype(BF16)
            back = dot(v_s[span, lanes], grads, NT)
            mean = jnp.sum(probs * back, axis=0, keepdims=True)
            inner = (probs * (back - mean)).astype(BF16)
            acc_v[span, :] = acc_v[span, :] + dot(low, grads)
            acc_k[span, :] = acc_k[span, :] + dot(inner, both)
            query = join_heads(dot(k_s[span, lanes], inner, TN)) * HEAD_DIM ** (-0.5)
            z_s[rows, lanes] = query.astype(BF16)

        loop(tiles, each)
        for k, acc in ((0, acc_k), (1, acc_v)):
            where = pl.ds(pl.multiple_of((k + 1) * D + pair * 128, 128), 128)
            z_s[:, where] = acc[pl.ds(offset, block), :].astype(BF16)
            halo_s[pair, k] = acc[pl.ds(outside, REACH), :].astype(BF16)
        halo(pair).start()

    loop(PAIRS, attend)

    def norm_one(i):
        rows = cols(i, 128)
        value = normal(tok[rows, :].astype(F32))[0]
        a2_s[rows, :] = (value * (1.0 + vecf[0:1, :]) + vecf[1:2, :]).astype(BF16)

    loop(block // 128, norm_one)
    weight_grad(a2_s, z_s.at[:, 0:D], 9)
    scatter.progress(7)

    def add_halo(pair):
        halo(pair).wait_recv()
        for k in range(2):
            where = pl.ds(pl.multiple_of((k + 1) * D + pair * 128, 128), 128)
            rows = pl.ds(away, REACH)
            z_s[rows, where] = (z_s[rows, where].astype(F32) + halo_r[pair, k].astype(F32)).astype(BF16)

    loop(PAIRS, add_halo)
    weight_grad(a2_s, z_s.at[:, D : 2 * D], 10)
    weight_grad(a2_s, z_s.at[:, 2 * D : 3 * D], 11)
    scatter.progress(8)
    for n in range(9, 12):
        take(n, lambda part: rows_from_stage(part, wbuf.at[pl.ds((n - 9) * D, D)], 0))

    def first_grad(n):
        value = None
        for t in range(3):
            rows = pl.ds(pl.multiple_of(t * D + n * 256, 256), 256)
            part = dot(z_s[:, t * D : t * D + D], wbuf[rows, :], NT)
            value = part if value is None else value + part
        x2_s[:, cols(n, 256)] = value

    loop(3, first_grad)
    scatter.progress(9)
    gain_row(2, slice(None), total_rows(z_s[:, 0:D]))
    gain_row(3, slice(None), total_rows(z_s[:, 2 * D : 3 * D]))

    def norm_first(i):
        rows = cols(i, 128)
        back, gain, shift = norm_back(tok[rows, :].astype(F32), x2_s[rows, :], vecf[0:1, :])
        tok_grad[rows, :] = (dx[rows, :] + back).astype(BF16)
        gain_row(0, slice(None), gain)
        gain_row(1, slice(None), shift)

    loop(block // 128, norm_first)
    vec.begin(0)
    for step in range(4):
        scatter.progress(10 + step)
        total = vec.total(step)
        if step < 3:
            vec_now[step + 1] = total
            vec.begin(step + 1)
        else:
            vec_out[...] = total
    scatter.progress(14)
    scatter.sent()
    vec.sent()
    loop(PAIRS, lambda pair: halo(pair).wait_send())


def backward_all(full, vec_low, tok, dy, seg_col, seg_row, *saved):
    block, near = tok.shape[0], seg_col.shape[0]
    tiles = block // TILE
    hbm, vmem = pl.BlockSpec(memory_space=pl.ANY), pl.BlockSpec(memory_space=pltpu.VMEM)
    vec_shape = vec_low.shape
    rows = (block, D)
    q, k, v, o, stat, x2, a2, act, slope = saved
    buffers = [
        ((C, Y, X, Z, NP) + PIECE, BF16),
        ((NP, Y, X, Z) + PIECE, BF16),
        ((NP, 2, 2, 2) + PIECE, BF16),
        ((NP, 2, 2) + PIECE, BF16),
        ((NP, Z - 1) + PIECE, BF16),
        ((4 * D, D), BF16),
        ((2, C, Y, X, Z) + PIECE, BF16),
        ((tiles, SPAN, TILE), F32),
        (vec_shape, F32),
        (rows, BF16),
        (rows, BF16),
        *[(array.shape, array.dtype) for array in saved],
        (rows, F32),
        (rows, BF16),
        ((near, 128), F32),
        ((near, 128), F32),
        ((PAIRS, 2, REACH, 128), BF16),
        ((PAIRS, 2, REACH, 128), BF16),
        ((4,) + vec_shape, F32),
        ((6,) + vec_shape, F32),
    ]
    semaphores = [(NP, 8), (NP, 8), (6,), (6,), (PAIRS,), (PAIRS,), (11,), (2,)]
    return pl.pallas_call(
        backward_kernel,
        out_shape=(
            jax.ShapeDtypeStruct((NP,) + PIECE, F32),
            jax.ShapeDtypeStruct(vec_shape, F32),
            jax.ShapeDtypeStruct(rows, BF16),
        ),
        in_specs=[hbm, vmem, hbm, hbm, vmem, vmem] + [hbm] * len(saved),
        out_specs=(vmem, vmem, vmem),
        scratch_shapes=[pltpu.VMEM(*one) for one in buffers] + [pltpu.SemaphoreType.DMA(one) for one in semaphores],
        compiler_params=pltpu.CompilerParams(
            collective_id=1, has_side_effects=True, vmem_limit_bytes=60 << 20
        ),
        name="backward_all",
    )(full, vec_low, tok, dy, seg_col, seg_row, *saved)


def from_pieces(pieces):
    count = pieces.shape[0]
    return pieces.reshape(count, 2, 24, 384).transpose(2, 0, 1, 3).reshape(24, count * 768)


def from_down(pieces):
    return pieces.reshape(2, 2, 48, 384).transpose(1, 2, 0, 3).reshape(96, 768)


def on_device_fast(
    tokens,
    segments,
    cotangent,
    qkv_weight,
    proj_weight,
    up_weight,
    down_weight,
    vec_params,
    qkv_velocity,
    proj_velocity,
    up_velocity,
    down_velocity,
    vec_velocity,
    qkv_average,
    proj_average,
    up_average,
    down_average,
    vec_average,
):
    block = tokens.shape[1]
    total_tokens = lax.axis_size("dp") * segments.shape[1]
    rate = 0.05 / math.sqrt(total_tokens)
    position = lax.axis_index("blk")
    shard = lax.axis_index("dp") * lax.axis_size("blk") + position
    unit = to_unit(*[w.astype(jnp.bfloat16) for w in (qkv_weight, proj_weight, up_weight, down_weight)])
    vec_placed = lax.dynamic_update_slice(
        jnp.zeros((16, D), jnp.bfloat16), vec_params.astype(jnp.bfloat16), (0, shard * vec_params.shape[1])
    )
    seg_near = lax.dynamic_slice_in_dim(segments, position * REACH, block + REACH, 1)
    seg_query = lax.dynamic_slice_in_dim(segments, position * block, block, 1)
    seg_col = jnp.broadcast_to(seg_near[0][:, None], (block + REACH, TILE))
    seg_row = jnp.broadcast_to(seg_query, (8, block))
    full, vec_low, result, *saved = forward_all(unit, vec_placed, tokens[0], seg_col, seg_row)
    pieces, vec_sum, back = backward_all(full, vec_low, tokens[0], cotangent[0], seg_col, seg_row, *saved)
    output, tokens_grad = result[None], back[None]
    query_share = from_pieces(pieces[9:12])
    proj_share = from_pieces(pieces[8:9])
    up_share = from_pieces(pieces[4:8])
    down_share = from_down(pieces[0:4])
    vec_share = lax.dynamic_slice(vec_sum, (0, shard * vec_params.shape[1]), vec_params.shape)
    qkv_new = update(qkv_weight, query_share, qkv_velocity, qkv_average, rate)
    proj_new = update(proj_weight, proj_share, proj_velocity, proj_average, rate)
    up_new = update(up_weight, up_share, up_velocity, up_average, rate)
    down_new = update(down_weight, down_share, down_velocity, down_average, rate)
    vec_new = update(vec_params, vec_share, vec_velocity, vec_average, rate)
    return (
        output,
        tokens_grad,
        query_share,
        proj_share,
        up_share,
        down_share,
        vec_share,
        qkv_new[0],
        proj_new[0],
        up_new[0],
        down_new[0],
        vec_new[0],
        qkv_new[1],
        proj_new[1],
        up_new[1],
        down_new[1],
        vec_new[1],
        qkv_new[2],
        proj_new[2],
        up_new[2],
        down_new[2],
        vec_new[2],
        qkv_new[0].astype(jnp.bfloat16),
        proj_new[0].astype(jnp.bfloat16),
        up_new[0].astype(jnp.bfloat16),
        down_new[0].astype(jnp.bfloat16),
        vec_new[0].astype(jnp.bfloat16),
    )


def solution(mesh):
    fits = mesh.shape["dp"] == Z * Y * C and mesh.shape["blk"] == X
    return jax.shard_map(
        on_device_fast if fits else on_device,
        mesh=mesh,
        in_specs=(
            P("dp", "blk", None),
            P("dp", None),
            P("dp", "blk", None),
            P(("dp", "blk"), None),
            P(("dp", "blk"), None),
            P(("dp", "blk"), None),
            P(("dp", "blk"), None),
            P(None, ("dp", "blk")),
            P(("dp", "blk"), None),
            P(("dp", "blk"), None),
            P(("dp", "blk"), None),
            P(("dp", "blk"), None),
            P(None, ("dp", "blk")),
            P(("dp", "blk"), None),
            P(("dp", "blk"), None),
            P(("dp", "blk"), None),
            P(("dp", "blk"), None),
            P(None, ("dp", "blk")),
        ),
        out_specs=(
            P("dp", "blk", None),
            P("dp", "blk", None),
            P(("dp", "blk"), None),
            P(("dp", "blk"), None),
            P(("dp", "blk"), None),
            P(("dp", "blk"), None),
            P(None, ("dp", "blk")),
            P(("dp", "blk"), None),
            P(("dp", "blk"), None),
            P(("dp", "blk"), None),
            P(("dp", "blk"), None),
            P(None, ("dp", "blk")),
            P(("dp", "blk"), None),
            P(("dp", "blk"), None),
            P(("dp", "blk"), None),
            P(("dp", "blk"), None),
            P(None, ("dp", "blk")),
            P(("dp", "blk"), None),
            P(("dp", "blk"), None),
            P(("dp", "blk"), None),
            P(("dp", "blk"), None),
            P(None, ("dp", "blk")),
            P(("dp", "blk"), None),
            P(("dp", "blk"), None),
            P(("dp", "blk"), None),
            P(("dp", "blk"), None),
            P(None, ("dp", "blk")),
        ),
        check_vma=False,
    )
```

profile of v0, /device:TPU:0, one launch (start us, length us, event | category | flops | bytes accessed | tf_op | source)
XLA Modules:
  0.0 238.0 jit_solution(17794711524428573271)
XLA Ops:
  0.7 0.7 copy-done
  1.4 0.7 convert_element_type.34
  2.1 0.6 broadcast_in_dim.27.seg_row
  3.0 0.9 convert_element_type.31
  3.9 1.0 convert_element_type.30
  5.0 1.0 convert_element_type.32
  6.1 1.0 convert_element_type.33
  7.3 0.9 broadcast_in_dim.25.seg_col
  8.2 104.4 %forward_all.1 = (bf16[2,2,2,4,12,48,384]{6,5,4,3,2,1,0:T(8,128)(2,1)}, bf16[16,768]{1,0:T(8,128)(2,1)}, bf16[512,768]{1,0:T(8,128)(2,1)}, bf16[512,768]{1,0:T(8...) custom-call(bf16[12,48,384]{2,1,0:T(8,128)(2,1)} %copy-done.12, ...), custom_call_target="tpu_custom_call" | custom-call | tf_op jit(solution)/shard_map/forward_all/pallas_call | solution.py:663
  112.7 109.9 %backward_all.1 = (f32[12,48,384]{2,1,0:T(8,128)}, f32[16,768]{1,0:T(8,128)}, bf16[512,768]{1,0:T(8,128)(2,1)}) custom-call(bf16[2,2,2,4,12,48,384]{6,5,4,3,2,1,0:T(8,128)(2,1)} %get-tuple-element.43.full, bf16[16,768]{1,0:T(8,128)(2,1)} %get-tuple-element.44.vec_in, bf16[512,768]{1,0:T(8,128)(2,1)} %bitcast.39, bf16[512,768]{1,0:T(8,128)(2,1)} %bitcast.48, ...), custom_call_target="tpu_custom_call" | custom-call | tf_op jit(solution)/shard_map/backward_all/pallas_call | solution.py:1058
  222.6 1.5 fusion
  224.7 0.9 slice.29
  225.7 0.7 fusion.3
  226.3 0.7 multiply_add_fusion.9
  227.0 0.9 slice.28
  228.0 1.1 fusion.5
  230.2 0.8 fusion.4
  231.1 1.8 multiply_add_fusion.6
  232.8 0.9 fusion.2
  233.7 0.8 multiply_add_fusion.1
  234.5 0.9 fusion.1
  235.4 0.8 multiply_add_fusion
  236.2 0.9 copy.64
  237.1 0.9 copy.65
  (83 shorter events, 2.4 us)
Async XLA Ops:
  3.0 5.2 %copy-start.21 = (bf16[16,768]{1,0:T(8,128)(2,1)}, bf16[16,768]{1,0:T(8,128)(2,1)S(1)}, u32[]{:S(2)}) copy-start(bf16[16,768]{1,0:T(8,128)(2,1)S(1)} %dynamic_update_slice.3.vec_in) | copy-start | bytes 73732
  112.6 110.0 %copy-start.25 = (f32[12,24]{1,0:T(8,128)S(1)}, f32[12,24]{1,0:T(8,128)}, u32[]{:S(2)}) copy-start(f32[12,24]{1,0:T(8,128)} %param.25) | copy-start | bytes 3460
  112.6 110.0 %copy-start.27 = (f32[12,24]{1,0:T(8,128)S(1)}, f32[12,24]{1,0:T(8,128)}, u32[]{:S(2)}) copy-start(f32[12,24]{1,0:T(8,128)} %param.30) | copy-start | bytes 3460
  112.6 111.4 %copy-start.26 = (f32[12,24]{1,0:T(8,128)S(1)}, f32[12,24]{1,0:T(8,128)}, u32[]{:S(2)}) copy-start(f32[12,24]{1,0:T(8,128)} %param.35) | copy-start | bytes 3460
  112.6 113.0 %copy-start.18 = (f32[24,768]{1,0:T(8,128)S(1)}, f32[24,768]{1,0:T(8,128)}, u32[]{:S(2)}) copy-start(f32[24,768]{1,0:T(8,128)} %param.22) | copy-start | bytes 221188
  112.7 113.0 %copy-start.22 = (f32[24,768]{1,0:T(8,128)S(1)}, f32[24,768]{1,0:T(8,128)}, u32[]{:S(2)}) copy-start(f32[24,768]{1,0:T(8,128)} %param.27) | copy-start | bytes 221188
  112.7 113.7 %copy-start.23 = (f32[24,768]{1,0:T(8,128)S(1)}, f32[24,768]{1,0:T(8,128)}, u32[]{:S(2)}) copy-start(f32[24,768]{1,0:T(8,128)} %param.32) | copy-start | bytes 221188
  222.5 7.6 %copy-start.8 = (f32[24,2304]{1,0:T(8,128)S(1)}, f32[24,2304]{1,0:T(8,128)}, u32[]{:S(2)}) copy-start(f32[24,2304]{1,0:T(8,128)} %param.21) | copy-start | bytes 663556
  222.6 7.6 %copy-start.20 = (f32[24,2304]{1,0:T(8,128)S(1)}, f32[24,2304]{1,0:T(8,128)}, u32[]{:S(2)}) copy-start(f32[24,2304]{1,0:T(8,128)} %param.26) | copy-start | bytes 663556
  224.1 7.0 %copy-start.24 = (f32[12,24]{1,0:T(8,128)}, f32[12,24]{1,0:T(8,128)S(1)}, u32[]{:S(2)}) copy-start(f32[12,24]{1,0:T(8,128)S(1)} %get-tuple-element.113) | copy-start | bytes 3460
  225.6 5.4 %copy-start.19 = (f32[3,8,2,384]{3,1,2,0:T(8,128)}, f32[3,8,2,384]{3,1,2,0:T(8,128)S(1)}, u32[]{:S(2)}) copy-start(f32[3,8,2,384]{3,1,2,0:T(8,128)S(1)} %copy.53) | copy-start | bytes 221188
  226.3 4.7 %copy-start.17 = (f32[24,768]{1,0:T(8,128)}, f32[24,768]{1,0:T(8,128)S(1)}, u32[]{:S(2)}) copy-start(f32[24,768]{1,0:T(8,128)S(1)} %get-tuple-element.110) | copy-start | bytes 221188
  227.9 4.9 %copy-start.3 = (f32[24,3072]{1,0:T(8,128)S(1)}, f32[24,3072]{1,0:T(8,128)}, u32[]{:S(2)}) copy-start(f32[24,3072]{1,0:T(8,128)} %param.23) | copy-start | bytes 884740
  228.0 4.9 %copy-start.13 = (f32[24,3072]{1,0:T(8,128)S(1)}, f32[24,3072]{1,0:T(8,128)}, u32[]{:S(2)}) copy-start(f32[24,3072]{1,0:T(8,128)} %param.28) | copy-start | bytes 884740
  229.4 4.3 %copy-start.14 = (f32[24,3072]{1,0:T(8,128)S(1)}, f32[24,3072]{1,0:T(8,128)}, u32[]{:S(2)}) copy-start(f32[24,3072]{1,0:T(8,128)} %param.33) | copy-start | bytes 884740
  229.4 5.1 %copy-start.5 = (f32[12,8,2,384]{3,1,2,0:T(8,128)}, f32[12,8,2,384]{3,1,2,0:T(8,128)S(1)}, u32[]{:S(2)}) copy-start(f32[12,8,2,384]{3,1,2,0:T(8,128)S(1)} %copy.54) | copy-start | bytes 884740
  229.4 5.1 %copy-start.4 = (f32[96,768]{1,0:T(8,128)S(1)}, f32[96,768]{1,0:T(8,128)}, u32[]{:S(2)}) copy-start(f32[96,768]{1,0:T(8,128)} %param.24) | copy-start | bytes 884740
  229.4 5.1 %copy-start.15 = (f32[96,768]{1,0:T(8,128)S(1)}, f32[96,768]{1,0:T(8,128)}, u32[]{:S(2)}) copy-start(f32[96,768]{1,0:T(8,128)} %param.29) | copy-start | bytes 884740
  229.8 5.5 %copy-start.6 = (f32[24,3072]{1,0:T(8,128)}, f32[24,3072]{1,0:T(8,128)S(1)}, u32[]{:S(2)}) copy-start(f32[24,3072]{1,0:T(8,128)S(1)} %reshape.115) | copy-start | bytes 884740
  230.0 5.4 %copy-start.16 = (f32[96,768]{1,0:T(8,128)S(1)}, f32[96,768]{1,0:T(8,128)}, u32[]{:S(2)}) copy-start(f32[96,768]{1,0:T(8,128)} %param.34) | copy-start | bytes 884740
  230.2 6.0 %copy-start.7 = (f32[24,2304]{1,0:T(8,128)}, f32[24,2304]{1,0:T(8,128)S(1)}, u32[]{:S(2)}) copy-start(f32[24,2304]{1,0:T(8,128)S(1)} %reshape.111) | copy-start | bytes 663556
  231.0 6.0 %copy-start.9 = (f32[24,2304]{1,0:T(8,128)}, f32[24,2304]{1,0:T(8,128)S(1)}, u32[]{:S(2)}) copy-start(f32[24,2304]{1,0:T(8,128)S(1)} %get-tuple-element.109) | copy-start | bytes 663556
  231.0 5.1 %copy-start.10 = (bf16[512,768]{1,0:T(8,128)(2,1)S(1)}, bf16[512,768]{1,0:T(8,128)(2,1)}, u32[]{:S(2)}) copy-start(bf16[512,768]{1,0:T(8,128)(2,1)} %get-tuple-element.42) | copy-start | bytes 2359300
  233.7 4.3 %copy-start.1 = (f32[24,3072]{1,0:T(8,128)}, f32[24,3072]{1,0:T(8,128)S(1)}, u32[]{:S(2)}) copy-start(f32[24,3072]{1,0:T(8,128)S(1)} %get-tuple-element.111) | copy-start | bytes 884740
  (4 other events, 8.5 us)
where the time goes:
time: 239 us; the launch traced here: 238 us
  Pallas kernels  214 us (90%)
  other arithmetic  13.8 us (6%)
  local copies, waits for them, and re-layouts  8.74 us (4%)
    pallas_call x1, Pallas kernels, backward_all(): pl.pallas_call(backward_kernel, out_shape=(jax.ShapeDtypeStruct((NP,) + P...  110 us
    pallas_call x1, Pallas kernels, forward_all(): pl.pallas_call(forward_kernel, out_shape=tuple((jax.ShapeDtypeStruct(*one...  104 us

commit v1 on v0

--- a/solution.py
+++ b/solution.py
@@ -1,3 +1,4 @@
+import functools
 import math
 
 import jax
@@ -252,9 +253,11 @@
 NP = 12
 Z, Y, X, C = 4, 2, 2, 2
 AHEAD = 2
-REACH = 256
 TILE = 128
+IMG_MAX = 198
+REACH = (IMG_MAX - 1 + 15) // 16 * 16
 SPAN = TILE + 2 * REACH
+GATHER_SPLIT = ((0, NP, 2),)
 PAIRS = HEADS // 2
 MESH = pl.DeviceIdType.MESH
 F32, BF16 = jnp.float32, jnp.bfloat16
@@ -363,18 +366,30 @@
     return cent * scale, scale
 
 
-def window(tile, x):
-    first = jnp.where(x == 0, jnp.maximum(tile - 2, 0), jnp.minimum(tile, 1))
-    return pl.ds(pl.multiple_of(first * TILE, TILE), SPAN)
-
-
-def mask_fill(seg_col, seg_row, bias, x, tiles):
-    def one(tile):
-        column = seg_col[window(tile, x), :]
-        row = seg_row[0:1, cols(tile, TILE)]
-        bias[tile] = jnp.where(column == row, 0.0, -1e30).astype(F32)
-
-    loop(tiles, one)
+def window_start(i, x, tiles):
+    near = tiles * TILE + REACH
+    first = max(i * TILE - REACH, 0)
+    count = min((i + 1) * TILE + REACH, near) - first
+    start = jnp.where(x == 0, first, near - first - count)
+    return jnp.where(x == 0, i, tiles - 1 - i), start, count
+
+
+def window(i, x, tiles):
+    tile, start, count = window_start(i, x, tiles)
+    return tile, pl.ds(pl.multiple_of(start, 16), count), count
+
+
+def mask_fill(seg, seg_col, bias, x, tiles):
+    length = seg.shape[1]
+    for k in range(length // TILE):
+        row = seg[0:1, k * TILE : k * TILE + TILE].astype(F32)
+        seg_col[k * TILE : k * TILE + TILE, :] = jnp.transpose(jnp.broadcast_to(row, (TILE, TILE)))
+    for i in range(tiles):
+        tile, start, count = window_start(i, x, tiles)
+        start = start + x * (length - tiles * TILE - REACH)
+        row = seg[0:1, pl.ds(pl.multiple_of((x * tiles + tile) * TILE, TILE), TILE)].astype(F32)
+        column = seg_col[pl.ds(pl.multiple_of(start, 16), count), :]
+        bias[i, 0:count] = jnp.where(column == row, 0.0, -1e30).astype(F32)
 
 
 def split_heads(pair_block):
@@ -390,22 +405,28 @@
     return jnp.transpose(own)
 
 
-def rows_from_stage(stage, target, col):
+def rows_from_stage(stage, target, t):
+    left, right = cols(2 * t, 384), cols(2 * t + 1, 384)
+
     def group(g):
         parts = [stage[c, g % Y, x, g // Y].astype(F32) for c in range(C) for x in range(X)]
         rows = pl.ds(pl.multiple_of(g * 96, 96), 96)
-        target[rows, col : col + 384] = jnp.concatenate([p[:24] for p in parts], axis=0).astype(BF16)
-        target[rows, col + 384 : col + 768] = jnp.concatenate([p[24:] for p in parts], axis=0).astype(BF16)
+        target[rows, left] = jnp.concatenate([p[:24] for p in parts], axis=0).astype(BF16)
+        target[rows, right] = jnp.concatenate([p[24:] for p in parts], axis=0).astype(BF16)
 
     loop(Z * Y, group)
 
 
-def down_from_stage(stage, target, half, col):
+def down_copies(full, target, t, sem):
+    half, col = (t - 8) % 2 * 48, (t - 8) // 2 * 384
+
     def group(g):
         for c in range(C):
             for x in range(X):
-                start = pl.multiple_of(g * 384 + (c * X + x) * 96 + half * 48, 16)
-                target[pl.ds(start, 48), col * 384 : col * 384 + 384] = stage[c, g % Y, x, g // Y]
+                row = pl.multiple_of(g * 384 + (c * X + x) * 96 + half, 16)
+                pltpu.make_async_copy(
+                    full.at[c, g % Y, x, g // Y, t], target.at[pl.ds(row, 48), col : col + 384], sem
+                ).start()
 
     loop(Z * Y, group)
 
@@ -428,20 +449,20 @@
             for k in range(1, Z)
         ]
 
-    def second(self, t):
+    def second(self, t, low):
         z, y, c, x = self.at
-        low, high = self.full.at[c, y, x, 0:2, t], self.full.at[c, y, x, 2:4, t]
+        one, two = self.full.at[c, y, x, 0:low, t], self.full.at[c, y, x, low:Z, t]
         return [
-            remote(low, low, self.send.at[t, 3], self.recv.at[t, 3], ident(z, y, c, 1 - x)),
-            remote(high, high, self.send.at[t, 4], self.recv.at[t, 4], ident(z, 1 - y, c, x)),
+            remote(one, one, self.send.at[t, 3], self.recv.at[t, 3], ident(z, y, c, 1 - x)),
+            remote(two, two, self.send.at[t, 4], self.recv.at[t, 4], ident(z, 1 - y, c, x)),
         ]
 
-    def third(self, t):
+    def third(self, t, low):
         z, y, c, x = self.at
-        low, high = self.full.at[c, y, :, 0:2, t], self.full.at[c, :, x, 2:4, t]
+        one, two = self.full.at[c, y, :, 0:low, t], self.full.at[c, :, x, low:Z, t]
         return [
-            remote(low, low, self.send.at[t, 5], self.recv.at[t, 5], ident(z, 1 - y, c, x)),
-            remote(high, high, self.send.at[t, 6], self.recv.at[t, 6], ident(z, y, c, 1 - x)),
+            remote(one, one, self.send.at[t, 5], self.recv.at[t, 5], ident(z, 1 - y, c, x)),
+            remote(two, two, self.send.at[t, 6], self.recv.at[t, 6], ident(z, y, c, 1 - x)),
         ]
 
     def last(self, t):
@@ -454,50 +475,65 @@
         loop(AHEAD, lambda t: begin(self.first(t)))
 
     def progress(self, i):
-        def to_second():
-            self.mine(i).wait()
-            arrive(self.first(i))
-            begin(self.second(i))
-
-        def to_third():
-            arrive(self.second(i - 1))
-            begin(self.third(i - 1))
-
-        def to_last():
-            arrive(self.third(i - 2))
-            begin(self.last(i - 2))
-
-        within(i, 0, NP, to_second)
-        within(i, 1, NP + 1, to_third)
-        within(i, 2, NP + 2, to_last)
-        within(i, 0, NP - AHEAD, lambda: begin(self.first(i + AHEAD)))
+        def to_second(t, low):
+            self.mine(t).wait()
+            arrive(self.first(t))
+            begin(self.second(t, low))
+
+        def to_third(t, low):
+            arrive(self.second(t, low))
+            begin(self.third(t, low))
+
+        def to_last(t, low):
+            arrive(self.third(t, low))
+            begin(self.last(t))
+
+        for first, end, low in GATHER_SPLIT:
+            within(i, first, end, lambda: to_second(i, low))
+        for first, end, low in GATHER_SPLIT:
+            within(i - 1, first, end, lambda: to_third(i - 1, low))
+        for first, end, low in GATHER_SPLIT:
+            within(i - 2, first, end, lambda: to_last(i - 2, low))
+        within(i + AHEAD, AHEAD, NP, lambda: begin(self.first(i + AHEAD)))
 
     def sent(self):
-        def one(t):
-            for copy in self.first(t) + self.second(t) + self.third(t) + self.last(t):
-                copy.wait_send()
-
-        loop(NP, one)
+        for first, end, low in GATHER_SPLIT:
+            def one(t):
+                for copy in self.first(t) + self.second(t, low) + self.third(t, low) + self.last(t):
+                    copy.wait_send()
+
+            lax.fori_loop(first, end, lambda t, carry: (one(t), carry)[1], 0)
 
 
 def forward_kernel(
-    unit, vec_in, tok, seg_col, seg_row,
-    full, vec_out, out_o, q_o, k_o, v_o, o_o, stat_o, x2_o, a2_o, z_o, slope_o,
-    near, a1, wbig, wdown, stage, vecf, bias, out_s, q_s, k_s, v_s, o_s, stat_s, x2_s, a2_s, z_s, slope_s,
-    vec_now, vec_got, own, send, recv, vsend, vrecv, hsem, ssem, osem,
+    w_qkv, w_proj, w_up, w_down, vec_in, tok, dy, seg,
+    full, vec_out, out_o, q_o, k_o, v_o, o_o, stat_o, x2_o, a2_o, z_o, slope_o, grad_o, bias_o,
+    unit, seg_col, near, a1, wbig, wdown, stage, vecf, bias, out_s, q_s, k_s, v_s, o_s, stat_s, x2_s, a2_s, z_s, slope_s, got,
+    local, vec_now, vec_got, own, send, recv, vsend, vrecv, hsem, ssem, dsem, osem, gsend, grecv,
 ):
     z, y, c, x = at = place()
     block = tok.shape[0]
     tiles = block // TILE
-    offset = pl.multiple_of(x * REACH, REACH)
+    offset = pl.multiple_of(x * REACH, 16)
     vec_now[0] = vec_in[...]
+
+    def pack(t, weight, j):
+        left, right = weight[:, j * 768 : j * 768 + 384], weight[:, j * 768 + 384 : j * 768 + 768]
+        unit[t] = jnp.concatenate([left, right], axis=0).astype(BF16)
+
+    for t, j in enumerate((1, 2, 0)):
+        pack(t, w_qkv, j)
+    pack(3, w_proj, 0)
+    for j in range(4):
+        pack(4 + j, w_up, j)
+        unit[8 + j] = w_down[j % 2 * 48 : j % 2 * 48 + 48, j // 2 * 384 : j // 2 * 384 + 384].astype(BF16)
     greet(*at)
     gather = Gather(at, unit, full, own, send, recv)
     gather.start()
     vec = Vec(at, vec_now, vec_got, vsend, vrecv)
     vec.begin(0)
-    away = pl.multiple_of((1 - x) * REACH, REACH)
-    land = pl.multiple_of(x * block, REACH)
+    away = pl.multiple_of((1 - x) * (block - REACH), 16)
+    land = pl.multiple_of(x * block, 16)
     halo = remote(
         tok.at[pl.ds(away, REACH)], near.at[pl.ds(land, REACH)], hsem.at[0], hsem.at[1], ident(z, y, c, 1 - x)
     )
@@ -516,50 +552,63 @@
             vec_out[...] = total
             vecf[...] = total.astype(F32)
 
-    def load(t):
+    def staged(t):
+        return pltpu.make_async_copy(full.at[:, :, :, :, t], stage.at[t % 4], ssem.at[t % 4])
+
+    def fetch(t):
         arrive(gather.last(t))
-        copy = pltpu.make_async_copy(full.at[:, :, :, :, t], stage, ssem)
-        copy.start()
-        copy.wait()
-
+        staged(t).start()
+
+    def take(t):
+        staged(t).wait()
+        rows_from_stage(stage.at[t % 4], wbig, t)
+
+    def down_start(t):
+        arrive(gather.last(t))
+        down_copies(full, wdown, t, dsem.at[t - 8])
+
+    def down_wait(t):
+        pltpu.make_async_copy(full.at[:, :, :, :, t], stage.at[0], dsem.at[t - 8]).wait()
+
+    gather.progress(0)
     vec_step(0)
+    gather.progress(1)
     vec_step(1)
-    gather.progress(0)
+    gather.progress(2)
     vec_step(2)
     vec_step(3)
-    gather.progress(1)
     halo.wait_recv()
 
     def norm_one(i):
-        rows = pl.ds(pl.multiple_of(i * 256, 256), 256)
+        rows = cols(i, 240)
         value = normal(near[rows, :].astype(F32))[0]
         a1[rows, :] = (value * (1.0 + vecf[0:1, :]) + vecf[1:2, :]).astype(BF16)
 
-    loop(near.shape[0] // 256, norm_one)
-    mask_fill(seg_col, seg_row, bias, x, tiles)
-    gather.progress(2)
+    loop(near.shape[0] // 240, norm_one)
+    mask_fill(seg, seg_col, bias, x, tiles)
+    put(11, bias, bias_o).start()
     gather.progress(3)
-    load(0)
-    rows_from_stage(stage, wbig, D)
+    fetch(0)
+    take(0)
 
     def keys(j):
-        k_s[:, cols(j, 256)] = dot(a1[...], wbig[:, pl.ds(pl.multiple_of(D + j * 256, 256), 256)]).astype(BF16)
+        k_s[:, cols(j, 256)] = dot(a1[...], wbig[:, cols(j, 256)]).astype(BF16)
 
     loop(3, keys)
     gather.progress(4)
-    load(1)
-    rows_from_stage(stage, wbig, 2 * D)
+    fetch(1)
+    take(1)
+    fetch(2)
 
     def values(j):
-        value = dot(a1[...], wbig[:, pl.ds(pl.multiple_of(2 * D + j * 256, 256), 256)])
-        v_s[:, cols(j, 256)] = (value + vecf[3:4, cols(j, 256)]).astype(BF16)
+        v_s[:, cols(j, 256)] = (dot(a1[...], wbig[:, cols(j + 3, 256)]) + vecf[3:4, cols(j, 256)]).astype(BF16)
 
     loop(3, values)
-    load(2)
-    rows_from_stage(stage, wbig, 0)
+    gather.progress(5)
+    take(2)
 
     def queries(j):
-        value = dot(a1[pl.ds(offset, block), :], wbig[:, cols(j, 256)]) + vecf[2:3, cols(j, 256)]
+        value = dot(a1[pl.ds(offset, block), :], wbig[:, cols(j + 6, 256)]) + vecf[2:3, cols(j, 256)]
         q_s[:, cols(j, 256)] = value.astype(BF16) * HEAD_DIM ** (-0.5)
 
     loop(3, queries)
@@ -568,32 +617,32 @@
     put(2, q_s, q_o).start()
 
     def attend(pair):
-        gather.progress(pair + 5)
+        pl.when(pair % 2 == 0)(lambda: gather.progress(6 + pair // 2))
+        pl.when(pair % 2 == 1)(lambda: fetch(3 + pair // 2))
         lanes = cols(pair, 128)
 
-        def one(tile):
+        for i in range(tiles):
+            tile, span, count = window(i, x, tiles)
             rows = cols(tile, TILE)
-            span = window(tile, x)
             both = split_heads(q_s[rows, lanes])
-            fill = bias[tile]
+            fill = bias[i, 0:count]
             scores = dot(k_s[span, lanes], both, NT) + jnp.concatenate([fill, fill], axis=1)
             top = jnp.max(scores, axis=0, keepdims=True)
             weights = jnp.exp(scores - top)
             total = jnp.sum(weights, axis=0, keepdims=True)
             mixed = dot(v_s[span, lanes], weights.astype(BF16), TN) / total
             o_s[rows, lanes] = join_heads(mixed).astype(BF16)
-            stat_s[pair * tiles + tile] = jnp.broadcast_to(top + jnp.log(total), (8, 2 * TILE))
-
-        loop(tiles, one)
+            stat_s[pair * tiles + i] = jnp.broadcast_to(top + jnp.log(total), (8, 2 * TILE))
+        pl.when(pair % 2 == 1)(lambda: take(3 + pair // 2))
 
     loop(PAIRS, attend)
     put(3, o_s, o_o).start()
     put(4, stat_s, stat_o).start()
-    load(3)
-    rows_from_stage(stage, wbig, 3 * D)
+    gather.progress(9)
+    fetch(6)
 
     def project(j):
-        value = dot(o_s[...], wbig[:, pl.ds(pl.multiple_of(3 * D + j * 256, 256), 256)])
+        value = dot(o_s[...], wbig[:, cols(j + 9, 256)])
         x2_s[:, cols(j, 256)] = tok[:, cols(j, 256)].astype(F32) + value + vecf[4:5, cols(j, 256)]
 
     loop(3, project)
@@ -606,44 +655,84 @@
     loop(block // 256, norm_two)
     put(5, x2_s, x2_o).start()
     put(6, a2_s, a2_o).start()
-    gather.progress(11)
+    gather.progress(10)
+    take(6)
+    fetch(7)
 
     def expand(j):
-        col = pl.multiple_of(j * 256, 256)
-        u = dot(a2_s[...], wbig[:, pl.ds(pl.multiple_of(4 * D + col, 256), 256)])
+        u = dot(a2_s[...], wbig[:, cols(j + 12, 256)])
         u = u + vecf[pl.ds(8 + j // 3, 1), pl.ds(pl.multiple_of((j % 3) * 256, 256), 256)]
         half = 0.5 + 0.5 * lax.erf(u * math.sqrt(0.5))
         z_s[:, cols(j, 256)] = (u * half).astype(BF16)
         slope = half + u * (jnp.exp(-0.5 * u * u) * (1.0 / math.sqrt(2.0 * math.pi)))
         slope_s[:, cols(j, 256)] = slope.astype(BF16)
 
-    for t in range(4):
-        load(4 + t)
-        rows_from_stage(stage, wbig, (4 + t) * D)
-        loop(3, lambda j: expand(j + 3 * t))
-        if t == 1:
-            gather.progress(12)
+    loop(5, expand)
+    gather.progress(11)
+    take(7)
+    loop(5, lambda j: expand(j + 5))
+    gather.progress(12)
+    down_start(8)
+    loop(2, lambda j: expand(j + 10))
     put(7, z_s, z_o).start()
     put(8, slope_s, slope_o).start()
-    gather.progress(13)
-    for t in range(4):
-        load(8 + t)
-        down_from_stage(stage, wdown, t % 2, t // 2)
-        if t % 2 == 1:
-            col = slice(t // 2 * 384, t // 2 * 384 + 384)
-            value = dot(z_s[...], wdown[:, col])
-            out_s[:, col] = (x2_s[:, col] + value + vecf[7:8, col]).astype(BF16)
+
+    def core(t):
+        peer = ident(z, y, 1 - c, x)
+        return remote(local.at[1 - c, :, :, :, t], got.at[t], gsend.at[t], grecv.at[t], peer)
+
+    for half in range(2):
+        def down_grad(g):
+            value = dot(z_s[:, cols(g, 384)], dy[:, half * 384 : half * 384 + 384], TN).astype(BF16)
+            for k in range(4):
+                for row in range(2):
+                    part = value[k * 96 + row * 48 : k * 96 + row * 48 + 48]
+                    local[k // 2, g % Y, k % 2, g // Y, 2 * half + row] = part
+
+        loop(Z * Y, down_grad)
+        core(2 * half).start()
+        core(2 * half + 1).start()
+        if half == 0:
+            gather.progress(13)
+            down_start(9)
+    down_start(10)
+
+    def contract(half):
+        col = slice(half * 384, half * 384 + 384)
+        value = dot(z_s[...], wdown[:, col])
+        out_s[:, col] = (x2_s[:, col] + value + vecf[7:8, col]).astype(BF16)
+
+    def gain(t):
+        core(t).wait_recv()
+        for a in range(Y):
+            for b in range(X):
+                own_part = local[c, a, b, :, t].astype(F32)
+                got[t, a, b] = (own_part + got[t, a, b].astype(F32)).astype(BF16)
+
+    loop(4, gain)
+    put(10, got, grad_o).start()
+    down_wait(8)
+    down_wait(9)
+    contract(0)
+    down_start(11)
+    down_wait(10)
+    down_wait(11)
+    contract(1)
     put(9, out_s, out_o).start()
     pairs = [(k_s, k_o), (v_s, v_o), (q_s, q_o), (o_s, o_o), (stat_s, stat_o), (x2_s, x2_o), (a2_s, a2_o)]
     for k, (src, dst) in enumerate(pairs + [(z_s, z_o), (slope_s, slope_o), (out_s, out_o)]):
         put(k, src, dst).wait()
+    put(10, got, grad_o).wait()
+    put(11, bias, bias_o).wait()
     gather.sent()
     vec.sent()
     halo.wait_send()
-
-
-def forward_all(unit, vec_placed, tok, seg_col, seg_row):
-    block, near = tok.shape[0], seg_col.shape[0]
+    loop(4, lambda t: core(t).wait_send())
+
+
+def forward_all(weights, vec_placed, tok, dy, seg):
+    block = tok.shape[0]
+    near = block + REACH
     ff = 4 * D
     tiles = block // TILE
     shapes = [
@@ -657,23 +746,27 @@
         ((block, D), BF16),
         ((block, ff), BF16),
         ((block, ff), BF16),
+        ((4, Y, X, Z) + PIECE, BF16),
+        ((tiles, SPAN, TILE), F32),
     ]
     hbm, vmem = pl.BlockSpec(memory_space=pl.ANY), pl.BlockSpec(memory_space=pltpu.VMEM)
     outs = [((C, Y, X, Z, NP) + PIECE, BF16), (vec_placed.shape, BF16)] + shapes
     return pl.pallas_call(
         forward_kernel,
         out_shape=tuple(jax.ShapeDtypeStruct(*one) for one in outs),
-        in_specs=[vmem] * 5,
+        in_specs=[vmem] * 8,
         out_specs=tuple([hbm, vmem] + [hbm] * len(shapes)),
         scratch_shapes=[
+            pltpu.VMEM((NP,) + PIECE, BF16),
+            pltpu.VMEM((seg.shape[1], TILE), F32),
             pltpu.VMEM((near, D), BF16),
             pltpu.VMEM((near, D), BF16),
             pltpu.VMEM((D, 8 * D), BF16),
             pltpu.VMEM((ff, D), BF16),
-            pltpu.VMEM((C, Y, X, Z) + PIECE, BF16),
+            pltpu.VMEM((4, C, Y, X, Z) + PIECE, BF16),
             pltpu.VMEM(vec_placed.shape, F32),
-            pltpu.VMEM((tiles, SPAN, TILE), F32),
-            *[pltpu.VMEM(*one) for one in shapes],
+            *[pltpu.VMEM(*one) for one in shapes[-1:] + shapes[:-1]],
+            pltpu.VMEM((C, Y, X, Z, 4) + PIECE, BF16),
             pltpu.VMEM((4,) + vec_placed.shape, BF16),
             pltpu.VMEM((6,) + vec_placed.shape, BF16),
             pltpu.SemaphoreType.DMA((NP,)),
@@ -682,25 +775,20 @@
             pltpu.SemaphoreType.DMA((6,)),
             pltpu.SemaphoreType.DMA((6,)),
             pltpu.SemaphoreType.DMA((2,)),
-            pltpu.SemaphoreType.DMA,
-            pltpu.SemaphoreType.DMA((10,)),
+            pltpu.SemaphoreType.DMA((4,)),
+            pltpu.SemaphoreType.DMA((4,)),
+            pltpu.SemaphoreType.DMA((12,)),
+            pltpu.SemaphoreType.DMA((4,)),
+            pltpu.SemaphoreType.DMA((4,)),
         ],
         compiler_params=pltpu.CompilerParams(
             collective_id=0, has_side_effects=True, vmem_limit_bytes=60 << 20
         ),
         name="forward_all",
-    )(unit, vec_placed, tok, seg_col, seg_row)
-
-
-def to_unit(qkv, proj, up, down):
-    def split(weight):
-        rows, width = weight.shape
-        count = width // 768
-        return weight.reshape(rows, count, 2, 384).transpose(1, 2, 0, 3).reshape(count, 48, 384)
-
-    three = split(qkv)
-    four = down.reshape(2, 48, 2, 384).transpose(2, 0, 1, 3).reshape(4, 48, 384)
-    return jnp.concatenate([three[1:], three[:1], split(proj), split(up), four], axis=0)
+    )(*weights, vec_placed, tok, dy, seg)
+
+
+SCATTER_SPLIT = ((0, 4, 3), (4, NP, 2))
 
 
 class Scatter:
@@ -711,22 +799,24 @@
     def core(self, t):
         z, y, c, x = self.at
         peer = ident(z, y, 1 - c, x)
-        return [remote(self.local.at[1 - c, :, :, :, t], self.got[0].at[t], self.send.at[t, 0], self.recv.at[t, 0], peer)]
-
-    def two(self, t):
+        return [remote(self.local.at[1 - c, :, :, :, t], self.got[0].at[t - 4], self.send.at[t, 0], self.recv.at[t, 0], peer)]
+
+    def two(self, t, low):
         z, y, c, x = self.at
-        low, high = self.local.at[c, 1 - y, :, 0:2, t], self.local.at[c, :, 1 - x, 2:4, t]
+        one, other = self.local.at[c, 1 - y, :, 0:low, t], self.local.at[c, :, 1 - x, low:Z, t]
+        got = self.got[1].at[t]
         return [
-            remote(low, self.got[1].at[t, 0], self.send.at[t, 1], self.recv.at[t, 1], ident(z, 1 - y, c, x)),
-            remote(high, self.got[1].at[t, 1], self.send.at[t, 2], self.recv.at[t, 2], ident(z, y, c, 1 - x)),
+            remote(one, got.at[:, 0:low], self.send.at[t, 1], self.recv.at[t, 1], ident(z, 1 - y, c, x)),
+            remote(other, got.at[:, low:Z], self.send.at[t, 2], self.recv.at[t, 2], ident(z, y, c, 1 - x)),
         ]
 
-    def one(self, t):
+    def one(self, t, low):
         z, y, c, x = self.at
-        low, high = self.local.at[c, y, 1 - x, 0:2, t], self.local.at[c, 1 - y, x, 2:4, t]
+        one, other = self.local.at[c, y, 1 - x, 0:low, t], self.local.at[c, 1 - y, x, low:Z, t]
+        got = self.got[2].at[t]
         return [
-            remote(low, self.got[2].at[t, 0], self.send.at[t, 3], self.recv.at[t, 3], ident(z, y, c, 1 - x)),
-            remote(high, self.got[2].at[t, 1], self.send.at[t, 4], self.recv.at[t, 4], ident(z, 1 - y, c, x)),
+            remote(one, got.at[0:low], self.send.at[t, 3], self.recv.at[t, 3], ident(z, y, c, 1 - x)),
+            remote(other, got.at[low:Z], self.send.at[t, 4], self.recv.at[t, 4], ident(z, 1 - y, c, x)),
         ]
 
     def along(self, t):
@@ -742,27 +832,29 @@
     def add(self, where, value):
         self.local[where] = (self.local[where].astype(F32) + value.astype(F32)).astype(BF16)
 
-    def after_core(self, t):
+    def take_core(self, t):
         c = self.at[2]
         arrive(self.core(t))
         for a in range(Y):
             for b in range(X):
-                self.add((c, a, b, slice(None), t), self.got[0][t, a, b])
-        begin(self.two(t))
-
-    def after_two(self, t):
+                self.add((c, a, b, slice(None), t), self.got[0][t - 4, a, b])
+
+    def after_core(self, t):
+        self.take_core(t)
+        self.go_two(t)
+
+    def after_two(self, t, low):
         z, y, c, x = self.at
-        arrive(self.two(t))
+        arrive(self.two(t, low))
         for b in range(2):
-            self.add((c, y, b, slice(0, 2), t), self.got[1][t, 0, b])
-            self.add((c, b, x, slice(2, 4), t), self.got[1][t, 1, b])
-        begin(self.one(t))
-
-    def after_one(self, t):
+            self.add((c, y, b, slice(0, low), t), self.got[1][t, b, 0:low])
+            self.add((c, b, x, slice(low, Z), t), self.got[1][t, b, low:Z])
+        begin(self.one(t, low))
+
+    def after_one(self, t, low):
         z, y, c, x = self.at
-        arrive(self.one(t))
-        for b in range(2):
-            self.add((c, y, x, slice(2 * b, 2 * b + 2), t), self.got[2][t, b])
+        arrive(self.one(t, low))
+        self.add((c, y, x, slice(None), t), self.got[2][t])
         begin(self.along(t))
 
     def after_z(self, t):
@@ -773,18 +865,27 @@
             total = total + self.got[3][t, k].astype(F32)
         self.out[t] = total
 
-    def progress(self, i):
-        within(i, 0, NP, lambda: self.after_core(i))
-        within(i, 1, NP + 1, lambda: self.after_two(i - 1))
-        within(i, 2, NP + 2, lambda: self.after_one(i - 2))
-        within(i, 3, NP + 3, lambda: self.after_z(i - 3))
+    def go_two(self, t):
+        for first, end, low in SCATTER_SPLIT:
+            within(t, first, end, lambda: begin(self.two(t, low)))
+
+    def go_one(self, t):
+        for first, end, low in SCATTER_SPLIT:
+            within(t, first, end, lambda: self.after_two(t, low))
+
+    def go_z(self, t):
+        arrive_one = self.after_one
+        for first, end, low in SCATTER_SPLIT:
+            within(t, first, end, lambda: arrive_one(t, low))
 
     def sent(self):
-        def each(t):
-            for copy in self.core(t) + self.two(t) + self.one(t) + self.along(t):
-                copy.wait_send()
-
-        loop(NP, each)
+        loop(NP - 4, lambda t: self.core(t + 4)[0].wait_send())
+        for first, end, low in SCATTER_SPLIT:
+            def each(t):
+                for copy in self.two(t, low) + self.one(t, low) + self.along(t):
+                    copy.wait_send()
+
+            lax.fori_loop(first, end, lambda t, carry: (each(t), carry)[1], 0)
 
 
 def total_rows(value):
@@ -801,18 +902,18 @@
 
 
 def backward_kernel(
-    full, vec_in, tok_o, dy_o, seg_col, seg_row, q_o, k_o, v_o, o_o, stat_o, x2_o, a2_o, z_o, slope_o,
+    full, vec_in, tok_o, dy_o, grad_o, bias_o, q_o, k_o, v_o, o_o, stat_o, x2_o, a2_o, slope_o,
     out, vec_out, tok_grad,
     local, got_core, got_two, got_one, got_z, wbuf, stage, bias, vecf, tok, dy, q_s, k_s, v_s, o_s, stat_s, x2_s, a2_s, z_s,
-    slope_s, dx, da, acc_k, acc_v, halo_s, halo_r, vec_now, vec_got, send, recv, vsend, vrecv, hsend, hrecv, isem, ssem,
+    slope_s, dx, da, acc_k, acc_v, halo_s, halo_r, vec_now, vec_got, send, recv, vsend, vrecv, hsend, hrecv, isem, ssem, dsem, gsem,
 ):
     z, y, c, x = at = place()
     block = tok.shape[0]
     tiles = block // TILE
-    offset = pl.multiple_of(x * REACH, REACH)
-    away = pl.multiple_of((1 - x) * REACH, REACH)
-    outside = pl.multiple_of((1 - x) * block, REACH)
-    order = [8, 9, 10, 11, 4, 5, 6, 7, 3, 2, 0, 1]
+    offset = pl.multiple_of(x * REACH, 16)
+    away = pl.multiple_of((1 - x) * (block - REACH), 16)
+    outside = pl.multiple_of((1 - x) * block, 16)
+    order = [4, 5, 6, 7, 3, 2, 0, 1]
 
     def fetch(n):
         return pltpu.make_async_copy(full.at[:, :, :, :, order[n]], stage.at[n % 2], ssem.at[n % 2])
@@ -820,28 +921,42 @@
     def take(n, use):
         fetch(n).wait()
         use(stage.at[n % 2])
-        if n + 2 < NP:
+        if n + 2 < len(order):
             fetch(n + 2).start()
 
     pairs = [
-        (z_o, z_s), (dy_o, dy), (slope_o, slope_s), (a2_o, a2_s), (x2_o, x2_s), (o_o, o_s), (k_o, k_s), (v_o, v_s),
-        (q_o, q_s), (stat_o, stat_s), (tok_o, tok),
+        (dy_o, dy), (slope_o, slope_s), (a2_o, a2_s), (x2_o, x2_s), (o_o, o_s), (k_o, k_s), (v_o, v_s), (q_o, q_s),
+        (stat_o, stat_s), (tok_o, tok), (bias_o, bias),
     ]
 
     def inward(k):
         return pltpu.make_async_copy(pairs[k][0], pairs[k][1], isem.at[k])
 
-    for k in range(2):
-        inward(k).start()
+    def grads(t):
+        return pltpu.make_async_copy(grad_o.at[t], local.at[c, :, :, :, t], gsem.at[t])
+
+    for t in range(4):
+        grads(t).start()
+    inward(0).start()
+    for t in range(8, 12):
+        down_copies(full, wbuf, t, dsem.at[t - 8])
     for n in range(2):
         fetch(n).start()
-    for k in range(2, len(pairs)):
+    for k in range(1, len(pairs)):
         inward(k).start()
     greet(*at)
     scatter = Scatter(at, local, got_core, got_two, got_one, got_z, out, send, recv)
     vec = Vec(at, vec_now, vec_got, vsend, vrecv)
     vec_now[0] = jnp.zeros(vec_now.shape[1:], F32)
     vecf[...] = vec_in[...].astype(F32)
+
+    def vec_step(step):
+        total = vec.total(step)
+        if step < 3:
+            vec_now[step + 1] = total
+            vec.begin(step + 1)
+        else:
+            vec_out[...] = total
 
     def gain_row(row, where, value):
         vec_now[0, row : row + 1, where] = vec_now[0, row : row + 1, where] + value
@@ -858,25 +973,14 @@
         loop(2, half)
         begin(scatter.core(t))
 
+    for t in range(4):
+        grads(t).wait()
+        scatter.go_two(t)
     inward(0).wait()
+    gain_row(7, slice(None), total_rows(dy[...]))
+    for t in range(8, 12):
+        pltpu.make_async_copy(full.at[:, :, :, :, t], stage.at[0], dsem.at[t - 8]).wait()
     inward(1).wait()
-    for col in range(2):
-        def down_grad(g):
-            value = dot(z_s[:, cols(g, 384)], dy[:, col * 384 : col * 384 + 384], TN).astype(BF16)
-            for k in range(4):
-                for half in range(2):
-                    part = value[k * 96 + half * 48 : k * 96 + half * 48 + 48]
-                    local[k // 2, g % Y, k % 2, g // Y, 2 * col + half] = part
-
-        loop(Z * Y, down_grad)
-        begin(scatter.core(2 * col))
-        begin(scatter.core(2 * col + 1))
-    gain_row(7, slice(None), total_rows(dy[...]))
-    mask_fill(seg_col, seg_row, bias, x, tiles)
-    for n in range(4):
-        take(n, lambda part: down_from_stage(part, wbuf, n % 2, n // 2))
-    inward(2).wait()
-    scatter.progress(0)
 
     def hidden(n):
         rows = pl.ds(pl.multiple_of(n * 256, 256), 256)
@@ -887,13 +991,16 @@
         vec_now[0, pl.ds(8 + n // 3, 1), where] = total_rows(low)
 
     loop(12, hidden)
-    scatter.progress(1)
-    inward(3).wait()
+    scatter.go_one(0)
+    inward(2).wait()
+    for t in range(2):
+        take(t, lambda part: rows_from_stage(part, wbuf.at[pl.ds(t * D, D)], 0))
     for t in range(4):
         weight_grad(a2_s, slope_s.at[:, t * D : t * D + D], 4 + t)
-    scatter.progress(2)
-    for n in range(4, 8):
-        take(n, lambda part: rows_from_stage(part, wbuf.at[pl.ds((n - 4) * D, D)], 0))
+    scatter.go_one(1)
+    scatter.go_one(2)
+    for t in range(2, 4):
+        take(t, lambda part: rows_from_stage(part, wbuf.at[pl.ds(t * D, D)], 0))
 
     def inner_grad(n):
         value = None
@@ -904,7 +1011,11 @@
         dx[:, cols(n, 256)] = value
 
     loop(3, inner_grad)
-    inward(4).wait()
+    scatter.after_core(4)
+    scatter.after_core(5)
+    scatter.go_one(3)
+    scatter.go_z(0)
+    inward(3).wait()
 
     def norm_two(i):
         rows = cols(i, 128)
@@ -919,17 +1030,20 @@
         gain_row(4, slice(None), total_rows(low))
 
     loop(block // 128, norm_two)
-    inward(5).wait()
+    scatter.after_core(6)
+    scatter.after_core(7)
+    scatter.go_z(1)
+    inward(4).wait()
     weight_grad(o_s, da, 8)
-    take(8, lambda part: rows_from_stage(part, wbuf.at[pl.ds(3 * D, D)], 0))
+    take(4, lambda part: rows_from_stage(part, wbuf.at[pl.ds(3 * D, D)], 0))
 
     def mixed_grad(n):
         rows = pl.ds(pl.multiple_of(3 * D + n * 256, 256), 256)
         o_s[:, cols(n, 256)] = dot(da[...], wbuf[rows, :], NT).astype(BF16)
 
     loop(3, mixed_grad)
-    scatter.progress(3)
-    for k in range(6, 11):
+    scatter.after_core(8)
+    for k in range(5, 11):
         inward(k).wait()
 
     def halo(pair):
@@ -937,17 +1051,19 @@
 
     def attend(pair):
         lanes = cols(pair, 128)
-        pl.when(pair % 2 == 1)(lambda: scatter.progress(4 + pair // 2))
+        scatter.go_z(2 + pair)
+        within(pair, 0, 5, lambda: scatter.go_one(4 + pair))
+        scatter.after_z(pair)
         acc_k[...] = jnp.zeros(acc_k.shape, F32)
         acc_v[...] = jnp.zeros(acc_v.shape, F32)
 
-        def each(tile):
+        for i in range(tiles):
+            tile, span, count = window(i, x, tiles)
             rows = cols(tile, TILE)
-            span = window(tile, x)
             both, grads = split_heads(q_s[rows, lanes]), split_heads(o_s[rows, lanes])
-            fill = bias[tile]
+            fill = bias[i, 0:count]
             scores = dot(k_s[span, lanes], both, NT) + jnp.concatenate([fill, fill], axis=1)
-            probs = jnp.exp(scores - stat_s[pair * tiles + tile][0:1])
+            probs = jnp.exp(scores - stat_s[pair * tiles + i][0:1])
             low = probs.astype(BF16)
             back = dot(v_s[span, lanes], grads, NT)
             mean = jnp.sum(probs * back, axis=0, keepdims=True)
@@ -957,7 +1073,6 @@
             query = join_heads(dot(k_s[span, lanes], inner, TN)) * HEAD_DIM ** (-0.5)
             z_s[rows, lanes] = query.astype(BF16)
 
-        loop(tiles, each)
         for k, acc in ((0, acc_k), (1, acc_v)):
             where = pl.ds(pl.multiple_of((k + 1) * D + pair * 128, 128), 128)
             z_s[:, where] = acc[pl.ds(offset, block), :].astype(BF16)
@@ -973,7 +1088,6 @@
 
     loop(block // 128, norm_one)
     weight_grad(a2_s, z_s.at[:, 0:D], 9)
-    scatter.progress(7)
 
     def add_halo(pair):
         halo(pair).wait_recv()
@@ -984,10 +1098,13 @@
 
     loop(PAIRS, add_halo)
     weight_grad(a2_s, z_s.at[:, D : 2 * D], 10)
+    scatter.after_core(9)
     weight_grad(a2_s, z_s.at[:, 2 * D : 3 * D], 11)
-    scatter.progress(8)
-    for n in range(9, 12):
-        take(n, lambda part: rows_from_stage(part, wbuf.at[pl.ds((n - 9) * D, D)], 0))
+    scatter.after_core(10)
+    scatter.go_z(8)
+    scatter.after_core(11)
+    for n in range(5, 8):
+        take(n, lambda part: rows_from_stage(part, wbuf.at[pl.ds((n - 5) * D, D)], 0))
 
     def first_grad(n):
         value = None
@@ -998,7 +1115,7 @@
         x2_s[:, cols(n, 256)] = value
 
     loop(3, first_grad)
-    scatter.progress(9)
+    scatter.go_one(9)
     gain_row(2, slice(None), total_rows(z_s[:, 0:D]))
     gain_row(3, slice(None), total_rows(z_s[:, 2 * D : 3 * D]))
 
@@ -1011,32 +1128,38 @@
 
     loop(block // 128, norm_first)
     vec.begin(0)
-    for step in range(4):
-        scatter.progress(10 + step)
-        total = vec.total(step)
-        if step < 3:
-            vec_now[step + 1] = total
-            vec.begin(step + 1)
-        else:
-            vec_out[...] = total
-    scatter.progress(14)
+    scatter.go_one(10)
+    scatter.go_z(9)
+    scatter.after_z(6)
+    vec_step(0)
+    scatter.go_one(11)
+    scatter.go_z(10)
+    scatter.after_z(7)
+    vec_step(1)
+    scatter.go_z(11)
+    scatter.after_z(8)
+    vec_step(2)
+    scatter.after_z(9)
+    vec_step(3)
+    scatter.after_z(10)
+    scatter.after_z(11)
     scatter.sent()
     vec.sent()
     loop(PAIRS, lambda pair: halo(pair).wait_send())
 
 
-def backward_all(full, vec_low, tok, dy, seg_col, seg_row, *saved):
-    block, near = tok.shape[0], seg_col.shape[0]
+def backward_all(full, vec_low, tok, dy, grad, fill, *saved):
+    block = tok.shape[0]
+    near = block + REACH
     tiles = block // TILE
     hbm, vmem = pl.BlockSpec(memory_space=pl.ANY), pl.BlockSpec(memory_space=pltpu.VMEM)
     vec_shape = vec_low.shape
     rows = (block, D)
-    q, k, v, o, stat, x2, a2, act, slope = saved
     buffers = [
         ((C, Y, X, Z, NP) + PIECE, BF16),
-        ((NP, Y, X, Z) + PIECE, BF16),
-        ((NP, 2, 2, 2) + PIECE, BF16),
-        ((NP, 2, 2) + PIECE, BF16),
+        ((NP - 4, Y, X, Z) + PIECE, BF16),
+        ((NP, 2, Z) + PIECE, BF16),
+        ((NP, Z) + PIECE, BF16),
         ((NP, Z - 1) + PIECE, BF16),
         ((4 * D, D), BF16),
         ((2, C, Y, X, Z) + PIECE, BF16),
@@ -1044,7 +1167,9 @@
         (vec_shape, F32),
         (rows, BF16),
         (rows, BF16),
-        *[(array.shape, array.dtype) for array in saved],
+        *[(array.shape, array.dtype) for array in saved[:-1]],
+        ((block, 3 * D), BF16),
+        ((block, 4 * D), BF16),
         (rows, F32),
         (rows, BF16),
         ((near, 128), F32),
@@ -1054,7 +1179,7 @@
         ((4,) + vec_shape, F32),
         ((6,) + vec_shape, F32),
     ]
-    semaphores = [(NP, 8), (NP, 8), (6,), (6,), (PAIRS,), (PAIRS,), (11,), (2,)]
+    semaphores = [(NP, 8), (NP, 8), (6,), (6,), (PAIRS,), (PAIRS,), (11,), (2,), (4,), (4,)]
     return pl.pallas_call(
         backward_kernel,
         out_shape=(
@@ -1062,23 +1187,52 @@
             jax.ShapeDtypeStruct(vec_shape, F32),
             jax.ShapeDtypeStruct(rows, BF16),
         ),
-        in_specs=[hbm, vmem, hbm, hbm, vmem, vmem] + [hbm] * len(saved),
+        in_specs=[hbm, vmem, hbm, hbm, hbm, hbm] + [hbm] * len(saved),
         out_specs=(vmem, vmem, vmem),
         scratch_shapes=[pltpu.VMEM(*one) for one in buffers] + [pltpu.SemaphoreType.DMA(one) for one in semaphores],
         compiler_params=pltpu.CompilerParams(
             collective_id=1, has_side_effects=True, vmem_limit_bytes=60 << 20
         ),
         name="backward_all",
-    )(full, vec_low, tok, dy, seg_col, seg_row, *saved)
-
-
-def from_pieces(pieces):
-    count = pieces.shape[0]
-    return pieces.reshape(count, 2, 24, 384).transpose(2, 0, 1, 3).reshape(24, count * 768)
-
-
-def from_down(pieces):
-    return pieces.reshape(2, 2, 48, 384).transpose(1, 2, 0, 3).reshape(96, 768)
+    )(full, vec_low, tok, dy, grad, fill, *saved)
+
+
+def update_kernel(rate, pieces, *refs):
+    masters, velocities, averages, grads, news, moving, means, copies = [refs[k : k + 4] for k in range(0, 32, 4)]
+
+    def one(k, rows, where, grad):
+        new, velocity, average = update(
+            masters[k][rows, where], grad, velocities[k][rows, where], averages[k][rows, where], rate
+        )
+        grads[k][rows, where] = grad
+        news[k][rows, where] = new
+        moving[k][rows, where] = velocity
+        means[k][rows, where] = average
+
+    for t in range(NP):
+        piece = pieces[t]
+        if t < 4:
+            one(3, slice(t % 2 * 48, t % 2 * 48 + 48), slice(t // 2 * 384, t // 2 * 384 + 384), piece)
+            continue
+        k, j = (2, t - 4) if t < 8 else (1, 0) if t == 8 else (0, t - 9)
+        for half in range(2):
+            col = (2 * j + half) * 384
+            one(k, slice(0, 24), slice(col, col + 384), piece[half * 24 : half * 24 + 24])
+    for k in range(4):
+        copies[k][...] = news[k][...].astype(BF16)
+
+
+def update_all(rate, pieces, masters, velocities, averages):
+    shapes = [jax.ShapeDtypeStruct(w.shape, F32) for w in masters] * 4
+    shapes += [jax.ShapeDtypeStruct(w.shape, BF16) for w in masters]
+    vmem = pl.BlockSpec(memory_space=pltpu.VMEM)
+    return pl.pallas_call(
+        functools.partial(update_kernel, rate),
+        out_shape=tuple(shapes),
+        in_specs=[vmem] * 13,
+        out_specs=tuple([vmem] * 20),
+        name="update_all",
+    )(pieces, *masters, *velocities, *averages)
 
 
 def on_device_fast(
@@ -1106,54 +1260,32 @@
     rate = 0.05 / math.sqrt(total_tokens)
     position = lax.axis_index("blk")
     shard = lax.axis_index("dp") * lax.axis_size("blk") + position
-    unit = to_unit(*[w.astype(jnp.bfloat16) for w in (qkv_weight, proj_weight, up_weight, down_weight)])
+    masters = (qkv_weight, proj_weight, up_weight, down_weight)
     vec_placed = lax.dynamic_update_slice(
         jnp.zeros((16, D), jnp.bfloat16), vec_params.astype(jnp.bfloat16), (0, shard * vec_params.shape[1])
     )
-    seg_near = lax.dynamic_slice_in_dim(segments, position * REACH, block + REACH, 1)
-    seg_query = lax.dynamic_slice_in_dim(segments, position * block, block, 1)
-    seg_col = jnp.broadcast_to(seg_near[0][:, None], (block + REACH, TILE))
-    seg_row = jnp.broadcast_to(seg_query, (8, block))
-    full, vec_low, result, *saved = forward_all(unit, vec_placed, tokens[0], seg_col, seg_row)
-    pieces, vec_sum, back = backward_all(full, vec_low, tokens[0], cotangent[0], seg_col, seg_row, *saved)
+    full, vec_low, result, *saved, act, slope, down, fill = forward_all(
+        masters, vec_placed, tokens[0], cotangent[0], segments
+    )
+    pieces, vec_sum, back = backward_all(full, vec_low, tokens[0], cotangent[0], down, fill, *saved, slope)
     output, tokens_grad = result[None], back[None]
-    query_share = from_pieces(pieces[9:12])
-    proj_share = from_pieces(pieces[8:9])
-    up_share = from_pieces(pieces[4:8])
-    down_share = from_down(pieces[0:4])
+    velocities = (qkv_velocity, proj_velocity, up_velocity, down_velocity)
+    averages = (qkv_average, proj_average, up_average, down_average)
+    done = update_all(rate, pieces, masters, velocities, averages)
     vec_share = lax.dynamic_slice(vec_sum, (0, shard * vec_params.shape[1]), vec_params.shape)
-    qkv_new = update(qkv_weight, query_share, qkv_velocity, qkv_average, rate)
-    proj_new = update(proj_weight, proj_share, proj_velocity, proj_average, rate)
-    up_new = update(up_weight, up_share, up_velocity, up_average, rate)
-    down_new = update(down_weight, down_share, down_velocity, down_average, rate)
     vec_new = update(vec_params, vec_share, vec_velocity, vec_average, rate)
     return (
         output,
         tokens_grad,
-        query_share,
-        proj_share,
-        up_share,
-        down_share,
+        *done[0:4],
         vec_share,
-        qkv_new[0],
-        proj_new[0],
-        up_new[0],
-        down_new[0],
+        *done[4:8],
         vec_new[0],
-        qkv_new[1],
-        proj_new[1],
-        up_new[1],
-        down_new[1],
+        *done[8:12],
         vec_new[1],
-        qkv_new[2],
-        proj_new[2],
-        up_new[2],
-        down_new[2],
+        *done[12:16],
         vec_new[2],
-        qkv_new[0].astype(jnp.bfloat16),
-        proj_new[0].astype(jnp.bfloat16),
-        up_new[0].astype(jnp.bfloat16),
-        down_new[0].astype(jnp.bfloat16),
+        *done[16:20],
         vec_new[0].astype(jnp.bfloat16),
     )
 

time: 239 us -> 208 us (0.87)
  Pallas kernels: 214 us -> 201 us
  other arithmetic: 13.8 us -> 2.77 us
  local copies, waits for them, and re-layouts: 8.74 us -> 2.73 us
    pallas_call x1, Pallas kernels: 110 us -> 97.7 us  [backward_all(): pl.pallas_call(backward_kernel, out_shape=(jax.ShapeDtypeStruct((NP,) + P...]
    convert_element_type x8 -> x0, other arithmetic: 7.01 us -> none  [the longest x4 3.81 us: on_device_fast(): w.astype(jnp.bfloat16)]
    pallas_call x1, Pallas kernels: 104 us -> 99.5 us  [forward_all(): pl.pallas_call(forward_kernel, out_shape=tuple((jax.ShapeDtypeStruct(*one...]
    pallas_call x0 -> x1, Pallas kernels: none -> 4.04 us  [update_all(): pl.pallas_call(functools.partial(update_kernel, rate), out_shape=tuple(sh...]
    add x5 -> x1, other arithmetic: 4.63 us -> 0.6 us  [update(): average_new = 0.9 * average + 0.1 * weight_new]
    slice x5 -> x0, local copies, waits for them, and re-layouts: 3 us -> none  [the longest x1 1.15 us: on_device_fast(): down_share = from_down(pieces[0:4])]
where the time goes in v1:
time: 208 us
  Pallas kernels  201 us (97%)
  other arithmetic  2.77 us (1%)
  local copies, waits for them, and re-layouts  2.73 us (1%)
    pallas_call x1, Pallas kernels, forward_all(): pl.pallas_call(forward_kernel, out_shape=tuple((jax.ShapeDtypeStruct(*one...  99.5 us
    pallas_call x1, Pallas kernels, backward_all(): pl.pallas_call(backward_kernel, out_shape=(jax.ShapeDtypeStruct((NP,) + P...  97.7 us

profile of v1, /device:TPU:0, one launch (start us, length us, event | category | flops | bytes accessed | tf_op | source)
XLA Modules:
  0.0 207.5 jit_solution(5628907014818938954)
XLA Ops:
  0.7 0.7 convert_element_type.6
  1.4 0.3 dynamic_update_slice.3.vec_in
  1.7 0.0 copy-start.2
  1.7 0.6 copy-done.2
  2.3 99.5 %forward_all.1 = (bf16[2,2,2,4,12,48,384]{6,5,4,3,2,1,0:T(8,128)(2,1)}, bf16[16,768]{1,0:T(8,128)(2,1)}, bf16[512,768]{1,0:T(8,128)(2,1)}, bf16[512,768]{1,0:T(8...) custom-call(f32[24,2304]{1,0:T(8,128)} %refs_0_.1, ...), custom_call_target="tpu_custom_call" | custom-call | tf_op jit(solution)/shard_map/forward_all/pallas_call | solution.py:754
  101.8 0.0 copy-start.4
  101.8 0.0 copy-start.6
  101.8 0.0 copy-start.5
  101.8 97.7 %backward_all.1 = (f32[12,48,384]{2,1,0:T(8,128)}, f32[16,768]{1,0:T(8,128)}, bf16[512,768]{1,0:T(8,128)(2,1)}) custom-call(bf16[2,2,2,4,12,48,384]{6,5,4,3,2,1,0:T(8,128)(2,1)} %get-tuple-element.64.full, bf16[16,768]{1,0:T(8,128)(2,1)} %get-tuple-element.65.vec_in, bf16[512,768]{1,0:T(8,128)(2,1)} %bitcast.5, bf16[512,768]{1,0:T(8,128)(2,1)} %bitcast.7, ...), custom_call_target="tpu_custom_call" | custom-call | tf_op jit(solution)/shard_map/backward_all/pallas_call | solution.py:1183
  199.6 0.0 copy-start
  199.6 0.0 copy-done.4
  199.6 0.0 copy-done.6
  199.6 1.5 fusion
  201.1 0.0 copy-start.3
  201.1 0.0 copy-done.5
  201.1 0.6 multiply_add_fusion
  201.7 0.0 copy-start.1
  201.7 4.0 %update_all.1 = (f32[24,2304]{1,0:T(8,128)}, f32[24,768]{1,0:T(8,128)}, f32[24,3072]{1,0:T(8,128)}, f32[96,768]{1,0:T(8,128)}, f32[24,2304]{1,0:T(8,128)}, /*ind...) custom-call(f32[12,48,384]{2,1,0:T(8,128)} %get-tuple-element.77.pie, ...), custom_call_target="tpu_custom_call" | custom-call | tf_op jit(solution)/shard_map/update_all/pallas_call | solution.py:1229
  205.7 0.0 copy-done
  205.7 0.9 copy.48
  206.6 0.0 copy-done.3
  206.6 0.0 copy-done.1
  206.6 0.9 copy.49
  (1 shorter events, 0.0 us)
Async XLA Ops:
  1.7 0.6 copy-start.2
  101.8 97.8 %copy-start.4 = (f32[12,24]{1,0:T(8,128)S(1)}, f32[12,24]{1,0:T(8,128)}, u32[]{:S(2)}) copy-start(f32[12,24]{1,0:T(8,128)} %param.25) | copy-start | bytes 3460
  101.8 97.8 %copy-start.6 = (f32[12,24]{1,0:T(8,128)S(1)}, f32[12,24]{1,0:T(8,128)}, u32[]{:S(2)}) copy-start(f32[12,24]{1,0:T(8,128)} %param.30) | copy-start | bytes 3460
  101.8 99.3 %copy-start.5 = (f32[12,24]{1,0:T(8,128)S(1)}, f32[12,24]{1,0:T(8,128)}, u32[]{:S(2)}) copy-start(f32[12,24]{1,0:T(8,128)} %param.35) | copy-start | bytes 3460
  199.6 6.2 %copy-start = (bf16[512,768]{1,0:T(8,128)(2,1)S(1)}, bf16[512,768]{1,0:T(8,128)(2,1)}, u32[]{:S(2)}) copy-start(bf16[512,768]{1,0:T(8,128)(2,1)} %get-tuple-element.63) | copy-start | bytes 2359300
  201.1 5.5 %copy-start.3 = (f32[12,24]{1,0:T(8,128)}, f32[12,24]{1,0:T(8,128)S(1)}, u32[]{:S(2)}) copy-start(f32[12,24]{1,0:T(8,128)S(1)} %get-tuple-element.141) | copy-start | bytes 3460
  201.7 4.9 %copy-start.1 = (bf16[512,768]{1,0:T(8,128)(2,1)S(1)}, bf16[512,768]{1,0:T(8,128)(2,1)}, u32[]{:S(2)}) copy-start(bf16[512,768]{1,0:T(8,128)(2,1)} %get-tuple-element.76) | copy-start | bytes 2359300

commit v2 on v1

--- a/solution.py
+++ b/solution.py
@@ -431,6 +431,12 @@
     loop(Z * Y, group)
 
 
+def qkv_columns(j, half):
+    if half == 0:
+        return (256 * j, 256), (D + 256 * j, 128)
+    return (D + 256 * j + 128, 128), (2 * D + 256 * j, 256)
+
+
 class Gather:
     def __init__(self, at, unit, full, own, send, recv):
         self.at, self.unit, self.full, self.own, self.send, self.recv = at, unit, full, own, send, recv
@@ -521,8 +527,12 @@
         left, right = weight[:, j * 768 : j * 768 + 384], weight[:, j * 768 + 384 : j * 768 + 768]
         unit[t] = jnp.concatenate([left, right], axis=0).astype(BF16)
 
-    for t, j in enumerate((1, 2, 0)):
-        pack(t, w_qkv, j)
+    for j in range(3):
+        sides = []
+        for half in range(2):
+            parts = [w_qkv[:, start : start + width] for start, width in qkv_columns(j, half)]
+            sides.append(jnp.concatenate(parts, axis=1))
+        unit[j] = jnp.concatenate(sides, axis=0).astype(BF16)
     pack(3, w_proj, 0)
     for j in range(4):
         pack(4 + j, w_up, j)
@@ -587,38 +597,7 @@
     loop(near.shape[0] // 240, norm_one)
     mask_fill(seg, seg_col, bias, x, tiles)
     put(11, bias, bias_o).start()
-    gather.progress(3)
-    fetch(0)
-    take(0)
-
-    def keys(j):
-        k_s[:, cols(j, 256)] = dot(a1[...], wbig[:, cols(j, 256)]).astype(BF16)
-
-    loop(3, keys)
-    gather.progress(4)
-    fetch(1)
-    take(1)
-    fetch(2)
-
-    def values(j):
-        v_s[:, cols(j, 256)] = (dot(a1[...], wbig[:, cols(j + 3, 256)]) + vecf[3:4, cols(j, 256)]).astype(BF16)
-
-    loop(3, values)
-    gather.progress(5)
-    take(2)
-
-    def queries(j):
-        value = dot(a1[pl.ds(offset, block), :], wbig[:, cols(j + 6, 256)]) + vecf[2:3, cols(j, 256)]
-        q_s[:, cols(j, 256)] = value.astype(BF16) * HEAD_DIM ** (-0.5)
-
-    loop(3, queries)
-    put(0, k_s, k_o).start()
-    put(1, v_s, v_o).start()
-    put(2, q_s, q_o).start()
-
     def attend(pair):
-        pl.when(pair % 2 == 0)(lambda: gather.progress(6 + pair // 2))
-        pl.when(pair % 2 == 1)(lambda: fetch(3 + pair // 2))
         lanes = cols(pair, 128)
 
         for i in range(tiles):
@@ -633,13 +612,31 @@
             mixed = dot(v_s[span, lanes], weights.astype(BF16), TN) / total
             o_s[rows, lanes] = join_heads(mixed).astype(BF16)
             stat_s[pair * tiles + i] = jnp.broadcast_to(top + jnp.log(total), (8, 2 * TILE))
-        pl.when(pair % 2 == 1)(lambda: take(3 + pair // 2))
-
-    loop(PAIRS, attend)
+
+    def third(j):
+        fetch(j)
+        gather.progress(3 + 2 * j)
+        take(j)
+        where = cols(j, 256)
+        value = dot(a1[pl.ds(offset, block), :], wbig[:, cols(3 * j, 256)]) + vecf[2:3, where]
+        q_s[:, where] = value.astype(BF16) * HEAD_DIM ** (-0.5)
+        k_s[:, where] = dot(a1[...], wbig[:, cols(3 * j + 1, 256)]).astype(BF16)
+        v_s[:, where] = (dot(a1[...], wbig[:, cols(3 * j + 2, 256)]) + vecf[3:4, where]).astype(BF16)
+        attend(2 * j)
+        gather.progress(4 + 2 * j)
+        attend(2 * j + 1)
+
+    loop(3, third)
+    put(0, k_s, k_o).start()
+    put(1, v_s, v_o).start()
+    put(2, q_s, q_o).start()
     put(3, o_s, o_o).start()
     put(4, stat_s, stat_o).start()
+    fetch(3)
+    take(3)
+    fetch(4)
+    fetch(5)
     gather.progress(9)
-    fetch(6)
 
     def project(j):
         value = dot(o_s[...], wbig[:, cols(j + 9, 256)])
@@ -656,7 +653,9 @@
     put(5, x2_s, x2_o).start()
     put(6, a2_s, a2_o).start()
     gather.progress(10)
-    take(6)
+    take(4)
+    take(5)
+    fetch(6)
     fetch(7)
 
     def expand(j):
@@ -669,6 +668,7 @@
 
     loop(5, expand)
     gather.progress(11)
+    take(6)
     take(7)
     loop(5, lambda j: expand(j + 5))
     gather.progress(12)
@@ -788,7 +788,7 @@
     )(*weights, vec_placed, tok, dy, seg)
 
 
-SCATTER_SPLIT = ((0, 4, 3), (4, NP, 2))
+SCATTER_SPLIT = ((0, NP, 2),)
 
 
 class Scatter:
@@ -913,7 +913,7 @@
     offset = pl.multiple_of(x * REACH, 16)
     away = pl.multiple_of((1 - x) * (block - REACH), 16)
     outside = pl.multiple_of((1 - x) * block, 16)
-    order = [4, 5, 6, 7, 3, 2, 0, 1]
+    order = [4, 5, 6, 7, 3, 0, 1, 2]
 
     def fetch(n):
         return pltpu.make_async_copy(full.at[:, :, :, :, order[n]], stage.at[n % 2], ssem.at[n % 2])
@@ -1049,6 +1049,9 @@
     def halo(pair):
         return remote(halo_s.at[pair], halo_r.at[pair], hsend.at[pair], hrecv.at[pair], ident(z, y, c, 1 - x))
 
+    def spot(pair, kind):
+        return pl.ds(pl.multiple_of(pair // 2 * D + kind * 256 + pair % 2 * 128, 128), 128)
+
     def attend(pair):
         lanes = cols(pair, 128)
         scatter.go_z(2 + pair)
@@ -1071,15 +1074,24 @@
             acc_v[span, :] = acc_v[span, :] + dot(low, grads)
             acc_k[span, :] = acc_k[span, :] + dot(inner, both)
             query = join_heads(dot(k_s[span, lanes], inner, TN)) * HEAD_DIM ** (-0.5)
-            z_s[rows, lanes] = query.astype(BF16)
+            z_s[rows, spot(pair, 0)] = query.astype(BF16)
 
         for k, acc in ((0, acc_k), (1, acc_v)):
-            where = pl.ds(pl.multiple_of((k + 1) * D + pair * 128, 128), 128)
-            z_s[:, where] = acc[pl.ds(offset, block), :].astype(BF16)
+            z_s[:, spot(pair, k + 1)] = acc[pl.ds(offset, block), :].astype(BF16)
             halo_s[pair, k] = acc[pl.ds(outside, REACH), :].astype(BF16)
         halo(pair).start()
 
-    loop(PAIRS, attend)
+    def add_halo(pair):
+        halo(pair).wait_recv()
+        for k in range(2):
+            where = spot(pair, k + 1)
+            rows = pl.ds(away, REACH)
+            z_s[rows, where] = (z_s[rows, where].astype(F32) + halo_r[pair, k].astype(F32)).astype(BF16)
+
+    def finish(j):
+        add_halo(2 * j)
+        add_halo(2 * j + 1)
+        weight_grad(a2_s, z_s.at[:, pl.ds(pl.multiple_of(j * D, D), D)], 9 + j)
 
     def norm_one(i):
         rows = cols(i, 128)
@@ -1087,19 +1099,14 @@
         a2_s[rows, :] = (value * (1.0 + vecf[0:1, :]) + vecf[1:2, :]).astype(BF16)
 
     loop(block // 128, norm_one)
-    weight_grad(a2_s, z_s.at[:, 0:D], 9)
-
-    def add_halo(pair):
-        halo(pair).wait_recv()
-        for k in range(2):
-            where = pl.ds(pl.multiple_of((k + 1) * D + pair * 128, 128), 128)
-            rows = pl.ds(away, REACH)
-            z_s[rows, where] = (z_s[rows, where].astype(F32) + halo_r[pair, k].astype(F32)).astype(BF16)
-
-    loop(PAIRS, add_halo)
-    weight_grad(a2_s, z_s.at[:, D : 2 * D], 10)
-    scatter.after_core(9)
-    weight_grad(a2_s, z_s.at[:, 2 * D : 3 * D], 11)
+
+    def third(j):
+        loop(2, lambda i: attend(2 * j + i))
+        within(j, 2, 3, lambda: scatter.after_core(9))
+        within(j, 1, 3, lambda: finish(j - 1))
+
+    loop(3, third)
+    finish(2)
     scatter.after_core(10)
     scatter.go_z(8)
     scatter.after_core(11)
@@ -1116,8 +1123,10 @@
 
     loop(3, first_grad)
     scatter.go_one(9)
-    gain_row(2, slice(None), total_rows(z_s[:, 0:D]))
-    gain_row(3, slice(None), total_rows(z_s[:, 2 * D : 3 * D]))
+    for j in range(3):
+        where = slice(j * 256, j * 256 + 256)
+        gain_row(2, where, total_rows(z_s[:, j * D : j * D + 256]))
+        gain_row(3, where, total_rows(z_s[:, j * D + 512 : j * D + 768]))
 
     def norm_first(i):
         rows = cols(i, 128)
@@ -1214,8 +1223,14 @@
         if t < 4:
             one(3, slice(t % 2 * 48, t % 2 * 48 + 48), slice(t // 2 * 384, t // 2 * 384 + 384), piece)
             continue
-        k, j = (2, t - 4) if t < 8 else (1, 0) if t == 8 else (0, t - 9)
+        k, j = (2, t - 4) if t < 8 else (1, 0)
         for half in range(2):
+            if t > 8:
+                part, col = piece[half * 24 : half * 24 + 24], 0
+                for start, width in qkv_columns(t - 9, half):
+                    one(0, slice(0, 24), slice(start, start + width), part[:, col : col + width])
+                    col += width
+                continue
             col = (2 * j + half) * 384
             one(k, slice(0, 24), slice(col, col + 384), piece[half * 24 : half * 24 + 24])
     for k in range(4):

time: 208 us -> 198 us (0.952)
  Pallas kernels: 201 us -> 191 us
    pallas_call x1, Pallas kernels: 99.5 us -> 94.1 us  [forward_all(): pl.pallas_call(forward_kernel, out_shape=tuple((jax.ShapeDtypeStruct(*one...]
    pallas_call x1, Pallas kernels: 97.7 us -> 92.9 us  [backward_all(): pl.pallas_call(backward_kernel, out_shape=(jax.ShapeDtypeStruct((NP,) + P...]
where the time goes in v2:
time: 198 us; the launch traced here: 197 us
  Pallas kernels  191 us (96%)
  other arithmetic  2.77 us (1%)
  local copies, waits for them, and re-layouts  2.73 us (1%)
    pallas_call x1, Pallas kernels, forward_all(): pl.pallas_call(forward_kernel, out_shape=tuple((jax.ShapeDtypeStruct(*one...  94.1 us
    pallas_call x1, Pallas kernels, backward_all(): pl.pallas_call(backward_kernel, out_shape=(jax.ShapeDtypeStruct((NP,) + P...  92.9 us
    pallas_call x1, Pallas kernels, update_all(): pl.pallas_call(functools.partial(update_kernel, rate), out_shape=tuple(sh...  4.04 us

profile of v2, /device:TPU:0, one launch (start us, length us, event | category | flops | bytes accessed | tf_op | source)
XLA Modules:
  0.0 197.3 jit_solution(16733322007299523460)
XLA Ops:
  0.7 0.7 convert_element_type.6
  1.4 0.3 dynamic_update_slice.3.vec_in
  1.7 0.0 copy-start.2
  1.7 0.6 copy-done.2
  2.3 94.1 %forward_all.1 = (bf16[2,2,2,4,12,48,384]{6,5,4,3,2,1,0:T(8,128)(2,1)}, bf16[16,768]{1,0:T(8,128)(2,1)}, bf16[512,768]{1,0:T(8,128)(2,1)}, bf16[512,768]{1,0:T(8...) custom-call(f32[24,2304]{1,0:T(8,128)} %refs_0_.1, ...), custom_call_target="tpu_custom_call" | custom-call | tf_op jit(solution)/shard_map/forward_all/pallas_call | solution.py:754
  96.4 0.0 copy-start.4
  96.4 0.0 copy-start.6
  96.4 0.0 copy-start.5
  96.4 92.9 %backward_all.1 = (f32[12,48,384]{2,1,0:T(8,128)}, f32[16,768]{1,0:T(8,128)}, bf16[512,768]{1,0:T(8,128)(2,1)}) custom-call(bf16[2,2,2,4,12,48,384]{6,5,4,3,2,1,0:T(8,128)(2,1)} %get-tuple-element.64.full, bf16[16,768]{1,0:T(8,128)(2,1)} %get-tuple-element.65.vec_in, bf16[512,768]{1,0:T(8,128)(2,1)} %bitcast.5, bf16[512,768]{1,0:T(8,128)(2,1)} %bitcast.7, ...), custom_call_target="tpu_custom_call" | custom-call | tf_op jit(solution)/shard_map/backward_all/pallas_call | solution.py:1192
  189.3 0.0 copy-start
  189.3 0.0 copy-done.4
  189.4 0.0 copy-done.6
  189.4 1.5 fusion
  190.8 0.0 copy-start.3
  190.8 0.0 copy-done.5
  190.8 0.6 multiply_add_fusion
  191.4 0.0 copy-start.1
  191.4 4.0 %update_all.1 = (f32[24,2304]{1,0:T(8,128)}, f32[24,768]{1,0:T(8,128)}, f32[24,3072]{1,0:T(8,128)}, f32[96,768]{1,0:T(8,128)}, f32[24,2304]{1,0:T(8,128)}, /*ind...) custom-call(f32[12,48,384]{2,1,0:T(8,128)} %get-tuple-element.77.pie, ...), custom_call_target="tpu_custom_call" | custom-call | tf_op jit(solution)/shard_map/update_all/pallas_call | solution.py:1244
  195.5 0.0 copy-done
  195.5 0.9 copy.48
  196.4 0.0 copy-done.3
  196.4 0.0 copy-done.1
  196.4 0.9 copy.49
  (1 shorter events, 0.0 us)
Async XLA Ops:
  1.7 0.6 copy-start.2
  96.4 93.0 %copy-start.4 = (f32[12,24]{1,0:T(8,128)S(1)}, f32[12,24]{1,0:T(8,128)}, u32[]{:S(2)}) copy-start(f32[12,24]{1,0:T(8,128)} %param.25) | copy-start | bytes 3460
  96.4 93.0 %copy-start.6 = (f32[12,24]{1,0:T(8,128)S(1)}, f32[12,24]{1,0:T(8,128)}, u32[]{:S(2)}) copy-start(f32[12,24]{1,0:T(8,128)} %param.30) | copy-start | bytes 3460
  96.4 94.4 %copy-start.5 = (f32[12,24]{1,0:T(8,128)S(1)}, f32[12,24]{1,0:T(8,128)}, u32[]{:S(2)}) copy-start(f32[12,24]{1,0:T(8,128)} %param.35) | copy-start | bytes 3460
  189.3 6.2 %copy-start = (bf16[512,768]{1,0:T(8,128)(2,1)S(1)}, bf16[512,768]{1,0:T(8,128)(2,1)}, u32[]{:S(2)}) copy-start(bf16[512,768]{1,0:T(8,128)(2,1)} %get-tuple-element.63) | copy-start | bytes 2359300
  190.8 5.5 %copy-start.3 = (f32[12,24]{1,0:T(8,128)}, f32[12,24]{1,0:T(8,128)S(1)}, u32[]{:S(2)}) copy-start(f32[12,24]{1,0:T(8,128)S(1)} %get-tuple-element.141) | copy-start | bytes 3460
  191.4 4.9 %copy-start.1 = (bf16[512,768]{1,0:T(8,128)(2,1)S(1)}, bf16[512,768]{1,0:T(8,128)(2,1)}, u32[]{:S(2)}) copy-start(bf16[512,768]{1,0:T(8,128)(2,1)} %get-tuple-element.76) | copy-start | bytes 2359300

commit v3 on v2

--- a/solution.py
+++ b/solution.py
@@ -280,7 +280,7 @@
     peers += [ident(z, 1 - y, c, x), ident(z, y, c, 1 - x), ident(z, y, 1 - c, x)]
     for peer in peers:
         pl.semaphore_signal(barrier, inc=1, device_id=peer, device_id_type=MESH)
-    pl.semaphore_wait(barrier, len(peers))
+    return lambda: pl.semaphore_wait(barrier, len(peers))
 
 
 def remote(src, dst, send, recv, peer):
@@ -515,12 +515,13 @@
     w_qkv, w_proj, w_up, w_down, vec_in, tok, dy, seg,
     full, vec_out, out_o, q_o, k_o, v_o, o_o, stat_o, x2_o, a2_o, z_o, slope_o, grad_o, bias_o,
     unit, seg_col, near, a1, wbig, wdown, stage, vecf, bias, out_s, q_s, k_s, v_s, o_s, stat_s, x2_s, a2_s, z_s, slope_s, got,
-    local, vec_now, vec_got, own, send, recv, vsend, vrecv, hsem, ssem, dsem, osem, gsend, grecv,
+    local, two, vec_now, vec_got, own, send, recv, vsend, vrecv, hsem, ssem, dsem, osem, gsend, grecv, tsend, trecv,
 ):
     z, y, c, x = at = place()
     block = tok.shape[0]
     tiles = block // TILE
     offset = pl.multiple_of(x * REACH, 16)
+    greeted = greet(*at)
     vec_now[0] = vec_in[...]
 
     def pack(t, weight, j):
@@ -537,7 +538,7 @@
     for j in range(4):
         pack(4 + j, w_up, j)
         unit[8 + j] = w_down[j % 2 * 48 : j % 2 * 48 + 48, j // 2 * 384 : j // 2 * 384 + 384].astype(BF16)
-    greet(*at)
+    greeted()
     gather = Gather(at, unit, full, own, send, recv)
     gather.start()
     vec = Vec(at, vec_now, vec_got, vsend, vrecv)
@@ -709,8 +710,19 @@
                 own_part = local[c, a, b, :, t].astype(F32)
                 got[t, a, b] = (own_part + got[t, a, b].astype(F32)).astype(BF16)
 
-    loop(4, gain)
-    put(10, got, grad_o).start()
+    def ahead(t):
+        along_y, along_x = ident(z, 1 - y, c, x), ident(z, y, c, 1 - x)
+        return [
+            remote(got.at[t, 1 - y, :, 0:2], two.at[t, :, 0:2], tsend.at[t, 0], trecv.at[t, 0], along_y),
+            remote(got.at[t, :, 1 - x, 2:Z], two.at[t, :, 2:Z], tsend.at[t, 1], trecv.at[t, 1], along_x),
+        ]
+
+    for t in range(4):
+        gain(t)
+        if t < 2:
+            begin(ahead(t))
+    late = pltpu.make_async_copy(got.at[2:4], grad_o.at[2:4], osem.at[10])
+    late.start()
     down_wait(8)
     down_wait(9)
     contract(0)
@@ -722,7 +734,18 @@
     pairs = [(k_s, k_o), (v_s, v_o), (q_s, q_o), (o_s, o_o), (stat_s, stat_o), (x2_s, x2_o), (a2_s, a2_o)]
     for k, (src, dst) in enumerate(pairs + [(z_s, z_o), (slope_s, slope_o), (out_s, out_o)]):
         put(k, src, dst).wait()
-    put(10, got, grad_o).wait()
+    for t in range(2):
+        arrive(ahead(t))
+        for b in range(2):
+            low, high = got[t, y, b, 0:2].astype(F32), got[t, b, x, 2:Z].astype(F32)
+            got[t, y, b, 0:2] = (low + two[t, b, 0:2].astype(F32)).astype(BF16)
+            got[t, b, x, 2:Z] = (high + two[t, b, 2:Z].astype(F32)).astype(BF16)
+        for copy in ahead(t):
+            copy.wait_send()
+    soon = pltpu.make_async_copy(got.at[0:2], grad_o.at[0:2], osem.at[12])
+    soon.start()
+    late.wait()
+    soon.wait()
     put(11, bias, bias_o).wait()
     gather.sent()
     vec.sent()
@@ -767,6 +790,7 @@
             pltpu.VMEM(vec_placed.shape, F32),
             *[pltpu.VMEM(*one) for one in shapes[-1:] + shapes[:-1]],
             pltpu.VMEM((C, Y, X, Z, 4) + PIECE, BF16),
+            pltpu.VMEM((2, 2, Z) + PIECE, BF16),
             pltpu.VMEM((4,) + vec_placed.shape, BF16),
             pltpu.VMEM((6,) + vec_placed.shape, BF16),
             pltpu.SemaphoreType.DMA((NP,)),
@@ -777,9 +801,11 @@
             pltpu.SemaphoreType.DMA((2,)),
             pltpu.SemaphoreType.DMA((4,)),
             pltpu.SemaphoreType.DMA((4,)),
-            pltpu.SemaphoreType.DMA((12,)),
+            pltpu.SemaphoreType.DMA((13,)),
             pltpu.SemaphoreType.DMA((4,)),
             pltpu.SemaphoreType.DMA((4,)),
+            pltpu.SemaphoreType.DMA((2, 2)),
+            pltpu.SemaphoreType.DMA((2, 2)),
         ],
         compiler_params=pltpu.CompilerParams(
             collective_id=0, has_side_effects=True, vmem_limit_bytes=60 << 20
@@ -882,8 +908,9 @@
         loop(NP - 4, lambda t: self.core(t + 4)[0].wait_send())
         for first, end, low in SCATTER_SPLIT:
             def each(t):
-                for copy in self.two(t, low) + self.one(t, low) + self.along(t):
+                for copy in self.one(t, low) + self.along(t):
                     copy.wait_send()
+                within(t, 2, NP, lambda: [copy.wait_send() for copy in self.two(t, low)] and None)
 
             lax.fori_loop(first, end, lambda t, carry: (each(t), carry)[1], 0)
 
@@ -908,6 +935,7 @@
     slope_s, dx, da, acc_k, acc_v, halo_s, halo_r, vec_now, vec_got, send, recv, vsend, vrecv, hsend, hrecv, isem, ssem, dsem, gsem,
 ):
     z, y, c, x = at = place()
+    greeted = greet(*at)
     block = tok.shape[0]
     tiles = block // TILE
     offset = pl.multiple_of(x * REACH, 16)
@@ -944,7 +972,7 @@
         fetch(n).start()
     for k in range(1, len(pairs)):
         inward(k).start()
-    greet(*at)
+    greeted()
     scatter = Scatter(at, local, got_core, got_two, got_one, got_z, out, send, recv)
     vec = Vec(at, vec_now, vec_got, vsend, vrecv)
     vec_now[0] = jnp.zeros(vec_now.shape[1:], F32)
@@ -975,7 +1003,10 @@
 
     for t in range(4):
         grads(t).wait()
-        scatter.go_two(t)
+        if t < 2:
+            begin(scatter.one(t, 2))
+        else:
+            scatter.go_two(t)
     inward(0).wait()
     gain_row(7, slice(None), total_rows(dy[...]))
     for t in range(8, 12):
@@ -991,14 +1022,14 @@
         vec_now[0, pl.ds(8 + n // 3, 1), where] = total_rows(low)
 
     loop(12, hidden)
-    scatter.go_one(0)
     inward(2).wait()
     for t in range(2):
         take(t, lambda part: rows_from_stage(part, wbuf.at[pl.ds(t * D, D)], 0))
     for t in range(4):
         weight_grad(a2_s, slope_s.at[:, t * D : t * D + D], 4 + t)
-    scatter.go_one(1)
+    scatter.after_core(4)
     scatter.go_one(2)
+    scatter.go_z(0)
     for t in range(2, 4):
         take(t, lambda part: rows_from_stage(part, wbuf.at[pl.ds(t * D, D)], 0))
 
@@ -1011,10 +1042,8 @@
         dx[:, cols(n, 256)] = value
 
     loop(3, inner_grad)
-    scatter.after_core(4)
     scatter.after_core(5)
     scatter.go_one(3)
-    scatter.go_z(0)
     inward(3).wait()
 
     def norm_two(i):
@@ -1206,8 +1235,10 @@
     )(full, vec_low, tok, dy, grad, fill, *saved)
 
 
-def update_kernel(rate, pieces, *refs):
+def update_kernel(rate, pieces, result, back, *refs):
     masters, velocities, averages, grads, news, moving, means, copies = [refs[k : k + 4] for k in range(0, 32, 4)]
+    refs[32][...] = result[...]
+    refs[33][...] = back[...]
 
     def one(k, rows, where, grad):
         new, velocity, average = update(
@@ -1237,17 +1268,18 @@
         copies[k][...] = news[k][...].astype(BF16)
 
 
-def update_all(rate, pieces, masters, velocities, averages):
+def update_all(rate, pieces, result, back, masters, velocities, averages):
     shapes = [jax.ShapeDtypeStruct(w.shape, F32) for w in masters] * 4
     shapes += [jax.ShapeDtypeStruct(w.shape, BF16) for w in masters]
+    shapes += [jax.ShapeDtypeStruct(result.shape, BF16), jax.ShapeDtypeStruct(back.shape, BF16)]
     vmem = pl.BlockSpec(memory_space=pltpu.VMEM)
     return pl.pallas_call(
         functools.partial(update_kernel, rate),
         out_shape=tuple(shapes),
-        in_specs=[vmem] * 13,
-        out_specs=tuple([vmem] * 20),
+        in_specs=[vmem] * 15,
+        out_specs=tuple([vmem] * 22),
         name="update_all",
-    )(pieces, *masters, *velocities, *averages)
+    )(pieces, result, back, *masters, *velocities, *averages)
 
 
 def on_device_fast(
@@ -1283,15 +1315,14 @@
         masters, vec_placed, tokens[0], cotangent[0], segments
     )
     pieces, vec_sum, back = backward_all(full, vec_low, tokens[0], cotangent[0], down, fill, *saved, slope)
-    output, tokens_grad = result[None], back[None]
     velocities = (qkv_velocity, proj_velocity, up_velocity, down_velocity)
     averages = (qkv_average, proj_average, up_average, down_average)
-    done = update_all(rate, pieces, masters, velocities, averages)
+    done = update_all(rate, pieces, result, back, masters, velocities, averages)
     vec_share = lax.dynamic_slice(vec_sum, (0, shard * vec_params.shape[1]), vec_params.shape)
     vec_new = update(vec_params, vec_share, vec_velocity, vec_average, rate)
     return (
-        output,
-        tokens_grad,
+        done[20][None],
+        done[21][None],
         *done[0:4],
         vec_share,
         *done[4:8],

time: 198 us -> 194 us (0.980)
  Pallas kernels: 191 us -> 189 us
    pallas_call x1, Pallas kernels: 92.9 us -> 87.5 us  [backward_all(): pl.pallas_call(backward_kernel, out_shape=(jax.ShapeDtypeStruct((NP,) + P...]
    pallas_call x1, Pallas kernels: 94.1 us -> 96.7 us  [forward_all(): pl.pallas_call(forward_kernel, out_shape=tuple((jax.ShapeDtypeStruct(*one...]
where the time goes in v3:
time: 194 us
  Pallas kernels  189 us (97%)
  other arithmetic  2.71 us (1%)
    pallas_call x1, Pallas kernels, forward_all(): pl.pallas_call(forward_kernel, out_shape=tuple((jax.ShapeDtypeStruct(*one...  96.7 us
    pallas_call x1, Pallas kernels, backward_all(): pl.pallas_call(backward_kernel, out_shape=(jax.ShapeDtypeStruct((NP,) + P...  87.5 us
    pallas_call x1, Pallas kernels, update_all(): pl.pallas_call(functools.partial(update_kernel, rate), out_shape=tuple(sh...  4.85 us

profile of v3, /device:TPU:0, one launch (start us, length us, event | category | flops | bytes accessed | tf_op | source)
XLA Modules:
  0.0 193.7 jit_solution(11702985923495279229)
XLA Ops:
  0.7 0.7 convert_element_type.6
  1.4 0.3 dynamic_update_slice.3.vec_in
  1.7 0.0 copy-start
  1.7 0.6 copy-done
  2.3 96.7 %forward_all.1 = (bf16[2,2,2,4,12,48,384]{6,5,4,3,2,1,0:T(8,128)(2,1)}, bf16[16,768]{1,0:T(8,128)(2,1)}, bf16[512,768]{1,0:T(8,128)(2,1)}, bf16[512,768]{1,0:T(8...) custom-call(f32[24,2304]{1,0:T(8,128)} %refs_0_.1, ...), custom_call_target="tpu_custom_call" | custom-call | tf_op jit(solution)/shard_map/forward_all/pallas_call | solution.py:777
  99.1 0.0 copy-start.2
  99.1 0.0 copy-start.4
  99.1 0.0 copy-start.3
  99.1 87.5 %backward_all.1 = (f32[12,48,384]{2,1,0:T(8,128)}, f32[16,768]{1,0:T(8,128)}, bf16[512,768]{1,0:T(8,128)(2,1)}) custom-call(bf16[2,2,2,4,12,48,384]{6,5,4,3,2,1,0:T(8,128)(2,1)} %get-tuple-element.65.full, bf16[16,768]{1,0:T(8,128)(2,1)} %get-tuple-element.66.vec_in, bf16[512,768]{1,0:T(8,128)(2,1)} %bitcast.5, bf16[512,768]{1,0:T(8,128)(2,1)} %bitcast.7, ...), custom_call_target="tpu_custom_call" | custom-call | tf_op jit(solution)/shard_map/backward_all/pallas_call | solution.py:1221
  186.6 0.0 copy-done.2
  186.6 0.0 copy-done.4
  186.7 1.4 fusion
  188.1 0.0 copy-start.1
  188.1 0.0 copy-done.3
  188.1 0.6 multiply_add_fusion
  188.7 4.8 %update_all.1 = (f32[24,2304]{1,0:T(8,128)}, f32[24,768]{1,0:T(8,128)}, f32[24,3072]{1,0:T(8,128)}, f32[96,768]{1,0:T(8,128)}, f32[24,2304]{1,0:T(8,128)}, /*ind...) custom-call(f32[12,48,384]{2,1,0:T(8,128)} %get-tuple-element.77.pie, ...), custom_call_target="tpu_custom_call" | custom-call | tf_op jit(solution)/shard_map/update_all/pallas_call | solution.py:1276
  193.5 0.0 copy-done.1
  (1 shorter events, 0.0 us)
Async XLA Ops:
  1.7 0.6 copy-start
  99.1 87.6 %copy-start.2 = (f32[12,24]{1,0:T(8,128)S(1)}, f32[12,24]{1,0:T(8,128)}, u32[]{:S(2)}) copy-start(f32[12,24]{1,0:T(8,128)} %param.25) | copy-start | bytes 3460
  99.1 87.6 %copy-start.4 = (f32[12,24]{1,0:T(8,128)S(1)}, f32[12,24]{1,0:T(8,128)}, u32[]{:S(2)}) copy-start(f32[12,24]{1,0:T(8,128)} %param.30) | copy-start | bytes 3460
  99.1 89.0 %copy-start.3 = (f32[12,24]{1,0:T(8,128)S(1)}, f32[12,24]{1,0:T(8,128)}, u32[]{:S(2)}) copy-start(f32[12,24]{1,0:T(8,128)} %param.35) | copy-start | bytes 3460
  188.1 5.5 %copy-start.1 = (f32[12,24]{1,0:T(8,128)}, f32[12,24]{1,0:T(8,128)S(1)}, u32[]{:S(2)}) copy-start(f32[12,24]{1,0:T(8,128)S(1)} %get-tuple-element.104) | copy-start | bytes 3460

commit v4 on v3

--- a/solution.py
+++ b/solution.py
@@ -717,15 +717,15 @@
             remote(got.at[t, :, 1 - x, 2:Z], two.at[t, :, 2:Z], tsend.at[t, 1], trecv.at[t, 1], along_x),
         ]
 
+    down_wait(8)
+    down_wait(9)
+    contract(0)
     for t in range(4):
         gain(t)
         if t < 2:
             begin(ahead(t))
     late = pltpu.make_async_copy(got.at[2:4], grad_o.at[2:4], osem.at[10])
     late.start()
-    down_wait(8)
-    down_wait(9)
-    contract(0)
     down_start(11)
     down_wait(10)
     down_wait(11)

time: 194 us -> 193 us (level)
  no operation moved by 1% of the time
where the time goes in v4:
time: 193 us
  Pallas kernels  188 us (97%)
  other arithmetic  2.71 us (1%)
    pallas_call x1, Pallas kernels, forward_all(): pl.pallas_call(forward_kernel, out_shape=tuple((jax.ShapeDtypeStruct(*one...  97 us
    pallas_call x1, Pallas kernels, backward_all(): pl.pallas_call(backward_kernel, out_shape=(jax.ShapeDtypeStruct((NP,) + P...  86.2 us
    pallas_call x1, Pallas kernels, update_all(): pl.pallas_call(functools.partial(update_kernel, rate), out_shape=tuple(sh...  4.85 us

profile of v4, /device:TPU:0, one launch (start us, length us, event | category | flops | bytes accessed | tf_op | source)
XLA Modules:
  0.0 192.6 jit_solution(1148921841571858806)
XLA Ops:
  0.7 0.7 convert_element_type.6
  1.4 0.3 dynamic_update_slice.3.vec_in
  1.7 0.0 copy-start
  1.7 0.6 copy-done
  2.3 97.0 %forward_all.1 = (bf16[2,2,2,4,12,48,384]{6,5,4,3,2,1,0:T(8,128)(2,1)}, bf16[16,768]{1,0:T(8,128)(2,1)}, bf16[512,768]{1,0:T(8,128)(2,1)}, bf16[512,768]{1,0:T(8...) custom-call(f32[24,2304]{1,0:T(8,128)} %refs_0_.1, ...), custom_call_target="tpu_custom_call" | custom-call | tf_op jit(solution)/shard_map/forward_all/pallas_call | solution.py:777
  99.3 0.0 copy-start.2
  99.4 0.0 copy-start.4
  99.4 0.0 copy-start.3
  99.4 86.2 %backward_all.1 = (f32[12,48,384]{2,1,0:T(8,128)}, f32[16,768]{1,0:T(8,128)}, bf16[512,768]{1,0:T(8,128)(2,1)}) custom-call(bf16[2,2,2,4,12,48,384]{6,5,4,3,2,1,0:T(8,128)(2,1)} %get-tuple-element.65.full, bf16[16,768]{1,0:T(8,128)(2,1)} %get-tuple-element.66.vec_in, bf16[512,768]{1,0:T(8,128)(2,1)} %bitcast.5, bf16[512,768]{1,0:T(8,128)(2,1)} %bitcast.7, ...), custom_call_target="tpu_custom_call" | custom-call | tf_op jit(solution)/shard_map/backward_all/pallas_call | solution.py:1221
  185.6 0.0 copy-done.2
  185.6 0.0 copy-done.4
  185.6 1.4 fusion
  187.0 0.0 copy-start.1
  187.0 0.0 copy-done.3
  187.0 0.6 multiply_add_fusion
  187.6 4.8 %update_all.1 = (f32[24,2304]{1,0:T(8,128)}, f32[24,768]{1,0:T(8,128)}, f32[24,3072]{1,0:T(8,128)}, f32[96,768]{1,0:T(8,128)}, f32[24,2304]{1,0:T(8,128)}, /*ind...) custom-call(f32[12,48,384]{2,1,0:T(8,128)} %get-tuple-element.77.pie, ...), custom_call_target="tpu_custom_call" | custom-call | tf_op jit(solution)/shard_map/update_all/pallas_call | solution.py:1276
  192.5 0.0 copy-done.1
  (1 shorter events, 0.0 us)
Async XLA Ops:
  1.7 0.6 copy-start
  99.3 86.2 %copy-start.2 = (f32[12,24]{1,0:T(8,128)S(1)}, f32[12,24]{1,0:T(8,128)}, u32[]{:S(2)}) copy-start(f32[12,24]{1,0:T(8,128)} %param.25) | copy-start | bytes 3460
  99.4 86.2 %copy-start.4 = (f32[12,24]{1,0:T(8,128)S(1)}, f32[12,24]{1,0:T(8,128)}, u32[]{:S(2)}) copy-start(f32[12,24]{1,0:T(8,128)} %param.30) | copy-start | bytes 3460
  99.4 87.6 %copy-start.3 = (f32[12,24]{1,0:T(8,128)S(1)}, f32[12,24]{1,0:T(8,128)}, u32[]{:S(2)}) copy-start(f32[12,24]{1,0:T(8,128)} %param.35) | copy-start | bytes 3460
  187.0 5.5 %copy-start.1 = (f32[12,24]{1,0:T(8,128)}, f32[12,24]{1,0:T(8,128)S(1)}, u32[]{:S(2)}) copy-start(f32[12,24]{1,0:T(8,128)S(1)} %get-tuple-element.104) | copy-start | bytes 3460

commit v5 on v4

--- a/solution.py
+++ b/solution.py
@@ -970,7 +970,7 @@
         down_copies(full, wbuf, t, dsem.at[t - 8])
     for n in range(2):
         fetch(n).start()
-    for k in range(1, len(pairs)):
+    for k in range(1, 3):
         inward(k).start()
     greeted()
     scatter = Scatter(at, local, got_core, got_two, got_one, got_z, out, send, recv)
@@ -1007,6 +1007,8 @@
             begin(scatter.one(t, 2))
         else:
             scatter.go_two(t)
+    for k in range(3, len(pairs)):
+        inward(k).start()
     inward(0).wait()
     gain_row(7, slice(None), total_rows(dy[...]))
     for t in range(8, 12):
@@ -1137,8 +1139,8 @@
     loop(3, third)
     finish(2)
     scatter.after_core(10)
+    scatter.after_core(11)
     scatter.go_z(8)
-    scatter.after_core(11)
     for n in range(5, 8):
         take(n, lambda part: rows_from_stage(part, wbuf.at[pl.ds((n - 5) * D, D)], 0))
 

time: 193 us -> 194 us (level)
  no operation moved by 1% of the time
where the time goes in v5:
time: 194 us; the launch traced here: 193 us
  Pallas kernels  188 us (97%)
  other arithmetic  2.71 us (1%)
    pallas_call x1, Pallas kernels, forward_all(): pl.pallas_call(forward_kernel, out_shape=tuple((jax.ShapeDtypeStruct(*one...  97 us
    pallas_call x1, Pallas kernels, backward_all(): pl.pallas_call(backward_kernel, out_shape=(jax.ShapeDtypeStruct((NP,) + P...  86.5 us
    pallas_call x1, Pallas kernels, update_all(): pl.pallas_call(functools.partial(update_kernel, rate), out_shape=tuple(sh...  4.85 us

profile of v5, /device:TPU:0, one launch (start us, length us, event | category | flops | bytes accessed | tf_op | source)
XLA Modules:
  0.0 193.0 jit_solution(13446567515334701424)
XLA Ops:
  0.7 0.7 convert_element_type.6
  1.4 0.3 dynamic_update_slice.3.vec_in
  1.7 0.0 copy-start
  1.7 0.6 copy-done
  2.3 97.0 %forward_all.1 = (bf16[2,2,2,4,12,48,384]{6,5,4,3,2,1,0:T(8,128)(2,1)}, bf16[16,768]{1,0:T(8,128)(2,1)}, bf16[512,768]{1,0:T(8,128)(2,1)}, bf16[512,768]{1,0:T(8...) custom-call(f32[24,2304]{1,0:T(8,128)} %refs_0_.1, ...), custom_call_target="tpu_custom_call" | custom-call | tf_op jit(solution)/shard_map/forward_all/pallas_call | solution.py:777
  99.3 0.0 copy-start.2
  99.4 0.0 copy-start.4
  99.4 0.0 copy-start.3
  99.4 86.5 %backward_all.1 = (f32[12,48,384]{2,1,0:T(8,128)}, f32[16,768]{1,0:T(8,128)}, bf16[512,768]{1,0:T(8,128)(2,1)}) custom-call(bf16[2,2,2,4,12,48,384]{6,5,4,3,2,1,0:T(8,128)(2,1)} %get-tuple-element.65.full, bf16[16,768]{1,0:T(8,128)(2,1)} %get-tuple-element.66.vec_in, bf16[512,768]{1,0:T(8,128)(2,1)} %bitcast.5, bf16[512,768]{1,0:T(8,128)(2,1)} %bitcast.7, ...), custom_call_target="tpu_custom_call" | custom-call | tf_op jit(solution)/shard_map/backward_all/pallas_call | solution.py:1223
  185.9 0.0 copy-done.2
  185.9 0.0 copy-done.4
  185.9 1.4 fusion
  187.3 0.0 copy-start.1
  187.3 0.0 copy-done.3
  187.3 0.6 multiply_add_fusion
  187.9 4.8 %update_all.1 = (f32[24,2304]{1,0:T(8,128)}, f32[24,768]{1,0:T(8,128)}, f32[24,3072]{1,0:T(8,128)}, f32[96,768]{1,0:T(8,128)}, f32[24,2304]{1,0:T(8,128)}, /*ind...) custom-call(f32[12,48,384]{2,1,0:T(8,128)} %get-tuple-element.77.pie, ...), custom_call_target="tpu_custom_call" | custom-call | tf_op jit(solution)/shard_map/update_all/pallas_call | solution.py:1278
  192.8 0.0 copy-done.1
  (1 shorter events, 0.0 us)
Async XLA Ops:
  1.7 0.6 copy-start
  99.3 86.6 %copy-start.2 = (f32[12,24]{1,0:T(8,128)S(1)}, f32[12,24]{1,0:T(8,128)}, u32[]{:S(2)}) copy-start(f32[12,24]{1,0:T(8,128)} %param.25) | copy-start | bytes 3460
  99.4 86.6 %copy-start.4 = (f32[12,24]{1,0:T(8,128)S(1)}, f32[12,24]{1,0:T(8,128)}, u32[]{:S(2)}) copy-start(f32[12,24]{1,0:T(8,128)} %param.30) | copy-start | bytes 3460
  99.4 88.0 %copy-start.3 = (f32[12,24]{1,0:T(8,128)S(1)}, f32[12,24]{1,0:T(8,128)}, u32[]{:S(2)}) copy-start(f32[12,24]{1,0:T(8,128)} %param.35) | copy-start | bytes 3460
  187.3 5.5 %copy-start.1 = (f32[12,24]{1,0:T(8,128)}, f32[12,24]{1,0:T(8,128)S(1)}, u32[]{:S(2)}) copy-start(f32[12,24]{1,0:T(8,128)S(1)} %get-tuple-element.104) | copy-start | bytes 3460
